TPU v7x, 32 devices: a whole 2x2x4 slice. The times are simulated.
32 devices in a mesh: orb: 4 (over z), pair: 8 (over y, x, core).
Axes of the slice: x: 2, y: 2, z: 4, core: 2. Of those that a mesh axis runs over, the one named last changes fastest.
Arguments:
- blocks: bfloat16 [128, 1024, 320], P(('orb', 'pair')), may hold values from -1.1953125 to 1.1953125
- aux_domain: int32 [128, 1024], replicated, may hold values from 0 to 2047, as said below
- pao_domain: int32 [128, 320], replicated, may hold values from -1 to 639, as said below
- pao_gap: float32 [128, 320], replicated, may hold values from 1 to 4
- amplitudes: bfloat16 [256, 320, 320], P(('orb', 'pair')), may hold values from -3 to 3
- pair_partner: int32 [256], replicated, may hold values from 0 to 127, as said below
- coupling_list: int32 [256, 4], P(('orb', 'pair')), may hold values from 0 to 255, as said below
- coupling_coef: float32 [256, 4], P(('orb', 'pair')), may hold values from -0.6 to 0.6
Outputs:
- new_amplitudes: bfloat16 [256, 320, 320], P(('orb', 'pair'))
- pair_energy: float32 [256], P(('orb', 'pair'))
- densities: float32 [128, 320, 320], P(('orb', 'pair'))
Inputs may be any that keep to these rules, and one draw needn't show every extreme that they name: `aux_domain`: each row holds 1024 distinct auxiliary function ids. `pao_domain`: each row holds distinct PAO ids in its leading slots and -1 in the rest; at least 160 ids a row. With d = p // 8, pair_partner[p] lies in [(d - 1) * 4, (d + 2) * 4). `coupling_list`: row p lists pair ids q with 0 < |q - p| <= 8.
All inputs are finite; a program needn't handle non-finite values.
Results may differ from a plain program's by a relative error of at most 0.003.
Values may be sent and summed in bfloat16 or wider, within the bound.
No kernel may reach another device: no remote copies, remote signals or barrier semaphores. Data moves between devices by JAX's collectives and lax.ppermute only.
A program may use at most 128 MiB of HBM per device.

v0:
```python
import jax
import jax.numpy as jnp
from jax import lax
from jax.sharding import PartitionSpec as P

OCC_DEV = 4
PAIR_DEV = 8


def with_halo(array, sides, width):
    for axis, dim in sides:
        peers, length = (lax.axis_size(axis), array.shape[dim])
        up = [(i, (i + 1) % peers) for i in range(peers - 1)]
        down = [(j, i) for i, j in up]
        last = lax.slice_in_dim(array, length - width, length, axis=dim)
        initial = lax.slice_in_dim(array, 0, width, axis=dim)
        before = lax.ppermute(last, axis, up)
        after = lax.ppermute(initial, axis, down)
        array = jnp.concatenate([before, array, after], axis=dim)
    return array


def passed_along(block, axis, distance):
    devices = range(lax.axis_size(axis))
    route = [(i - distance, i) for i in devices if i - distance in devices]
    return lax.ppermute(block, axis, route)


def first_orbital(pair_id):
    return pair_id // PAIR_DEV * OCC_DEV + pair_id % OCC_DEV


def selector(wanted, present):
    equal = (wanted[:, None] == present[None, :]) & (wanted[:, None] >= 0)
    return equal.astype(jnp.bfloat16)


def pair_terms(
    left_block,
    right_block,
    aux_left,
    aux_right,
    pao_left,
    pao_right,
    gap_left,
    gap_right,
    amp,
    near_amps,
    near_left,
    near_right,
    coefs,
):
    aligned = jnp.dot(
        selector(aux_left, aux_right), right_block, preferred_element_type=jnp.float32
    ).astype(jnp.bfloat16)
    mask_left = (pao_left >= 0).astype(jnp.float32)
    mask_right = (pao_right >= 0).astype(jnp.float32)
    both = mask_left[:, None] * mask_right[None, :]
    exchange = (
        lax.dot_general(
            left_block, aligned, (((0,), (0,)), ((), ())), preferred_element_type=jnp.float32
        )
        * both
    )
    masked = (amp.astype(jnp.float32) * both).astype(jnp.bfloat16)

    def project(near_amp, pao_near_left, pao_near_right, coef):
        rows = jnp.dot(
            selector(pao_left, pao_near_left), near_amp, preferred_element_type=jnp.float32
        ).astype(jnp.bfloat16)
        picked = lax.dot_general(
            rows,
            selector(pao_right, pao_near_right),
            (((1,), (1,)), ((), ())),
            preferred_element_type=jnp.float32,
        )
        return coef * picked

    coupling = jnp.sum(jax.vmap(project)(near_amps, near_left, near_right, coefs), axis=0)
    denom = gap_left[:, None] + gap_right[None, :]
    masked_f = masked.astype(jnp.float32)
    residual = exchange + denom * masked_f - coupling
    new_amp = (masked_f - 0.5 * residual / denom).astype(jnp.bfloat16)
    energy = jnp.sum(exchange * masked_f) / masked.shape[0]
    return (new_amp, energy, masked)


def left_density(masked):
    return (
        lax.dot_general(
            masked, masked, (((1,), (1,)), ((), ())), preferred_element_type=jnp.float32
        )
        / masked.shape[0]
    )


def right_density(masked):
    return (
        lax.dot_general(
            masked, masked, (((0,), (0,)), ((), ())), preferred_element_type=jnp.float32
        )
        / masked.shape[0]
    )


def local(
    blocks, aux_domain, pao_domain, pao_gap, amplitudes, pair_partner, coupling_list, coupling_coef
):
    here = lax.axis_index(("orb", "pair"))
    occ_local = blocks.shape[0]
    pairs_local = amplitudes.shape[0]
    width = amplitudes.shape[1]
    wide_blocks = with_halo(blocks, ((("orb", "pair"), 0),), occ_local)
    wide_amps = with_halo(amplitudes, ((("orb", "pair"), 0),), pairs_local)
    orbital_base = (here - 1) * occ_local
    pair_base = (here - 1) * pairs_local
    local_ids = here * pairs_local + jnp.arange(pairs_local, dtype=jnp.int32)

    def one_pair(items):
        pair_id, amp, neighbours, coefs = items
        left = first_orbital(pair_id)
        right = pair_partner[pair_id]
        left_block = lax.dynamic_index_in_dim(wide_blocks, left - orbital_base, 0, keepdims=False)
        right_block = lax.dynamic_index_in_dim(wide_blocks, right - orbital_base, 0, keepdims=False)
        near_amps = jnp.take(wide_amps, neighbours - pair_base, axis=0)
        near_left = pao_domain[first_orbital(neighbours)]
        near_right = pao_domain[pair_partner[neighbours]]
        new_amp, energy, masked = pair_terms(
            left_block,
            right_block,
            aux_domain[left],
            aux_domain[right],
            pao_domain[left],
            pao_domain[right],
            pao_gap[left],
            pao_gap[right],
            amp,
            near_amps,
            near_left,
            near_right,
            coefs,
        )
        return (new_amp, energy, masked, left_density(masked))

    new_amps, energies, masked_all, left_terms = lax.map(
        one_pair, (local_ids, amplitudes, coupling_list, coupling_coef)
    )
    densities = jnp.sum(
        left_terms.reshape(pairs_local // occ_local, occ_local, width, width), axis=0
    )
    right_terms = lax.map(right_density, masked_all)
    spots = pair_partner[local_ids] - orbital_base
    table = (spots[:, None] == jnp.arange(3 * occ_local)[None, :]).astype(jnp.float32)
    spread = jnp.einsum("pe,pab->eab", table, right_terms, precision=lax.Precision.HIGHEST)
    from_before = passed_along(
        spread[2 * occ_local :].astype(jnp.bfloat16), ("orb", "pair"), 1
    ).astype(jnp.float32)
    from_after = passed_along(spread[:occ_local].astype(jnp.bfloat16), ("orb", "pair"), -1).astype(
        jnp.float32
    )
    densities = densities + spread[occ_local : 2 * occ_local] + from_before + from_after
    return (new_amps, energies, densities)


def solution(mesh):
    return jax.shard_map(
        local,
        mesh=mesh,
        in_specs=(
            P(("orb", "pair"), None, None),
            P(),
            P(),
            P(),
            P(("orb", "pair"), None, None),
            P(),
            P(("orb", "pair"), None),
            P(("orb", "pair"), None),
        ),
        out_specs=(
            P(("orb", "pair"), None, None),
            P(("orb", "pair")),
            P(("orb", "pair"), None, None),
        ),
        check_vma=False,
    )
```

profile of v0, /device:TPU:1, one launch (start us, length us, event | category | flops | bytes accessed | tf_op | source)
XLA Modules:
  0.0 470.5 jit_solution(9563126728292916379)
XLA Ops:
  0.6 4.5 collective-permute-start
  5.1 1.9 collective-permute-start.1
  7.1 3.6 collective-permute-start.2
  10.7 2.0 collective-permute-start.3
  17.8 86.5 %collective-permute-done.2 = bf16[8,320,320]{2,1,0:T(8,128)(2,1)} collective-permute-done((bf16[8,320,320]{2,1,0:T(8,128)(2,1)}, bf16[8,320,320]{2,1,0:T(8,128)(2,1)}, u32[]{:S(2)}, u32[]{:S(2)}) %collective-permute-start.2) | collective-permute-done | bytes 1638432 | tf_op jit(solution)/shard_map/ppermute | solution.py:17
  105.9 6.7 %pad_maximum_fusion.1 = bf16[24,320,320]{2,1,0:T(8,128)(2,1)} fusion(bf16[8,320,320]{2,1,0:T(8,128)(2,1)} %collective-permute-done.3, bf16[8,320,320]{2,1,0:T(8,128)(2,1)} %param.16, bf16[8,320,320]{2,1,0:T(8,128)(2,1)} %collective-permute-done.2), kind=kLoop, calls=%fused_computation.104 | loop fusion | flops 4915200 | bytes 9830400 | tf_op jit(solution)/shard_map/concatenate | solution.py:19
  112.6 5.6 %pad_maximum_fusion = bf16[12,1024,320]{1,2,0:T(8,128)(2,1)} fusion(bf16[4,1024,320]{1,2,0:T(8,128)(2,1)} %collective-permute-done.1, bf16[4,1024,320]{1,2,0:T(8,128)(2,1)S(1)} %copy-done.1, bf16[4,1024,320]{1,2,0:T(8,128)(2,1)S(1)} %collective-permute-done), kind=kLoop, calls=%fused_computation.103 | loop fusion | flops 7864320 | bytes 15728640 | tf_op jit(solution)/shard_map/concatenate | solution.py:19
  118.2 11.6 %copy.29 = bf16[12,1024,320]{2,1,0:T(8,128)(2,1)} copy(bf16[12,1024,320]{1,2,0:T(8,128)(2,1)} %pad_maximum_fusion) | data formatting | bytes 15728640 | tf_op jit(solution)/shard_map/while | solution.py:145
  129.8 194.1 %while.29 = (s32[]{:T(128)}, bf16[8,320,320]{2,1,0:T(8,128)(2,1)}, f32[8]{0:T(128)S(1)}, bf16[8,320,320]{2,1,0:T(8,128)(2,1)}, f32[8,320,320]{2,1,0:T(8,128)}, /...) while((s32[]{:T(128)}, bf16[8,320,320]{2,1,0:T(8,128)(2,1)}, ...), condition=%wide.region_3.4_spmd, body=%wide.region_0.3_spmd.sunk | while | flops 1479203584 | bytes 7548515 | solution.py:145
  138.3 3.4 gather_fusion.2
  145.4 3.9 fusion.125
  151.8 2.3 fusion.127
  162.6 3.4 gather_fusion.2
  169.7 3.9 fusion.125
  176.1 2.2 fusion.127
  186.8 3.4 gather_fusion.2
  194.0 3.9 fusion.125
  200.4 2.2 fusion.127
  211.1 3.4 gather_fusion.2
  218.2 3.9 fusion.125
  224.7 2.3 fusion.127
  235.4 3.4 gather_fusion.2
  242.5 3.9 fusion.125
  248.9 2.2 fusion.127
  259.6 3.4 gather_fusion.2
  266.7 3.9 fusion.125
  273.1 2.3 fusion.127
  283.9 3.4 gather_fusion.2
  291.0 3.9 fusion.125
  297.4 2.3 fusion.127
  308.1 3.4 gather_fusion.2
  315.3 3.9 fusion.125
  321.7 2.2 fusion.127
  324.5 105.8 %while.30 = (s32[]{:T(128)}, f32[8,320,320]{2,0,1:T(8,128)}, bf16[8,320,320]{2,1,0:T(8,128)(2,1)}, s32[]{:T(128)}, s32[]{:T(128)}) while((s32[]{:T(128)}, f32[8,320,320]{2,0,1:T(8,128)}, bf16[8,320,320]{2,1,0:T(8,128)(2,1)}, s32[]{:T(128)}, s32[]{:T(128)}) %tuple.85), condition=%wide.region_6.7_spmd, body=%wide.region_5.6_spmd.sunk | while | flops 65638400 | bytes 2294337 | solution.py:151
  326.4 11.3 %dynamic_update_slice.44 = f32[8,320,320]{2,0,1:T(8,128)} dynamic-update-slice(f32[8,320,320]{2,0,1:T(8,128)} %get-tuple-element.659, f32[1,320,320]{2,0,1:T(1,128)S(1)} %copy.41, s32[]{:T(128)} %get-tuple-element.658, s32[]{:T(128)} %constant.204.clone.1..sunk.1, s32[]{:T(128)} %constant.204.clone.1..sunk.1) | dynamic-update-slice | bytes 819204 | tf_op jit(solution)/shard_map/while/body/jit(dynamic_update_index_in_dim)/dynamic_update_slice | solution.py:145
  339.6 11.3 %dynamic_update_slice.44 = f32[8,320,320]{2,0,1:T(8,128)} dynamic-update-slice(f32[8,320,320]{2,0,1:T(8,128)} %get-tuple-element.659, f32[1,320,320]{2,0,1:T(1,128)S(1)} %copy.41, s32[]{:T(128)} %get-tuple-element.658, s32[]{:T(128)} %constant.204.clone.1..sunk.1, s32[]{:T(128)} %constant.204.clone.1..sunk.1) | dynamic-update-slice | bytes 819204 | tf_op jit(solution)/shard_map/while/body/jit(dynamic_update_index_in_dim)/dynamic_update_slice | solution.py:145
  352.9 11.3 %dynamic_update_slice.44 = f32[8,320,320]{2,0,1:T(8,128)} dynamic-update-slice(f32[8,320,320]{2,0,1:T(8,128)} %get-tuple-element.659, f32[1,320,320]{2,0,1:T(1,128)S(1)} %copy.41, s32[]{:T(128)} %get-tuple-element.658, s32[]{:T(128)} %constant.204.clone.1..sunk.1, s32[]{:T(128)} %constant.204.clone.1..sunk.1) | dynamic-update-slice | bytes 819204 | tf_op jit(solution)/shard_map/while/body/jit(dynamic_update_index_in_dim)/dynamic_update_slice | solution.py:145
  366.1 11.3 %dynamic_update_slice.44 = f32[8,320,320]{2,0,1:T(8,128)} dynamic-update-slice(f32[8,320,320]{2,0,1:T(8,128)} %get-tuple-element.659, f32[1,320,320]{2,0,1:T(1,128)S(1)} %copy.41, s32[]{:T(128)} %get-tuple-element.658, s32[]{:T(128)} %constant.204.clone.1..sunk.1, s32[]{:T(128)} %constant.204.clone.1..sunk.1) | dynamic-update-slice | bytes 819204 | tf_op jit(solution)/shard_map/while/body/jit(dynamic_update_index_in_dim)/dynamic_update_slice | solution.py:145
  379.3 11.3 %dynamic_update_slice.44 = f32[8,320,320]{2,0,1:T(8,128)} dynamic-update-slice(f32[8,320,320]{2,0,1:T(8,128)} %get-tuple-element.659, f32[1,320,320]{2,0,1:T(1,128)S(1)} %copy.41, s32[]{:T(128)} %get-tuple-element.658, s32[]{:T(128)} %constant.204.clone.1..sunk.1, s32[]{:T(128)} %constant.204.clone.1..sunk.1) | dynamic-update-slice | bytes 819204 | tf_op jit(solution)/shard_map/while/body/jit(dynamic_update_index_in_dim)/dynamic_update_slice | solution.py:145
  392.5 11.3 %dynamic_update_slice.44 = f32[8,320,320]{2,0,1:T(8,128)} dynamic-update-slice(f32[8,320,320]{2,0,1:T(8,128)} %get-tuple-element.659, f32[1,320,320]{2,0,1:T(1,128)S(1)} %copy.41, s32[]{:T(128)} %get-tuple-element.658, s32[]{:T(128)} %constant.204.clone.1..sunk.1, s32[]{:T(128)} %constant.204.clone.1..sunk.1) | dynamic-update-slice | bytes 819204 | tf_op jit(solution)/shard_map/while/body/jit(dynamic_update_index_in_dim)/dynamic_update_slice | solution.py:145
  405.8 11.3 %dynamic_update_slice.44 = f32[8,320,320]{2,0,1:T(8,128)} dynamic-update-slice(f32[8,320,320]{2,0,1:T(8,128)} %get-tuple-element.659, f32[1,320,320]{2,0,1:T(1,128)S(1)} %copy.41, s32[]{:T(128)} %get-tuple-element.658, s32[]{:T(128)} %constant.204.clone.1..sunk.1, s32[]{:T(128)} %constant.204.clone.1..sunk.1) | dynamic-update-slice | bytes 819204 | tf_op jit(solution)/shard_map/while/body/jit(dynamic_update_index_in_dim)/dynamic_update_slice | solution.py:145
  419.0 11.3 %dynamic_update_slice.44 = f32[8,320,320]{2,0,1:T(8,128)} dynamic-update-slice(f32[8,320,320]{2,0,1:T(8,128)} %get-tuple-element.659, f32[1,320,320]{2,0,1:T(1,128)S(1)} %copy.41, s32[]{:T(128)} %get-tuple-element.658, s32[]{:T(128)} %constant.204.clone.1..sunk.1, s32[]{:T(128)} %constant.204.clone.1..sunk.1) | dynamic-update-slice | bytes 819204 | tf_op jit(solution)/shard_map/while/body/jit(dynamic_update_index_in_dim)/dynamic_update_slice | solution.py:145
  430.3 7.1 %fusion.94 = (bf16[12,320,320]{2,0,1:T(8,128)(2,1)S(1)}, f32[12,320,320]{2,0,1:T(8,128)}) fusion(f32[8,320,320]{2,0,1:T(8,128)} %get-tuple-element.285, s32[8]{0:T(128)S(1)} %broadcast_subtract_fusion), kind=kOutput, calls=%fused_computation.119 | convolution fusion | flops 119193696 | bytes 10649632 | tf_op jit(solution)/shard_map/pe,pab->eab/dot_general | solution.py:154
  439.3 2.5 collective-permute-start.4
  441.9 2.1 collective-permute-start.5
  444.0 2.7 reduce_sum.35
  446.6 17.1 %collective-permute-done.4 = bf16[4,320,320]{2,0,1:T(4,128)(2,1)S(1)} collective-permute-done((bf16[4,320,320]{2,0,1:T(4,128)(2,1)}, bf16[4,320,320]{2,0,1:T(4,128)(2,1)S(1)}, u32[]{:S(2)}, u32[]{:S(2)}) %collective-permute-start.4) | collective-permute-done | bytes 819232 | tf_op jit(solution)/shard_map/ppermute | solution.py:26
  464.6 4.4 fusion.82
  (202 shorter events, 86.5 us)
Async XLA Ops:
  0.6 112.0 %collective-permute-start = (bf16[4,1024,320]{1,2,0:T(8,128)(2,1)}, bf16[4,1024,320]{1,2,0:T(8,128)(2,1)S(1)}, u32[]{:S(2)}, u32[]{:S(2)}) collective-permute-start(bf16[4,1024,320]{1,2,0:T(8,128)(2,1)} %param.12), channel_id=1, source_target_pairs={{0,1},{1,2},{2,3},{3,4},{4,5},{5,6},{6,7},{7,8},{8,9},{9,10},{10,1... | collective-permute-start | bytes 7864328 | tf_op jit(solution)/shard_map/ppermute | solution.py:17
  5.1 107.4 %collective-permute-start.1 = (bf16[4,1024,320]{1,2,0:T(8,128)(2,1)}, bf16[4,1024,320]{1,2,0:T(8,128)(2,1)}, u32[]{:S(2)}, u32[]{:S(2)}) collective-permute-start(bf16[4,1024,320]{1,2,0:T(8,128)(2,1)} %param.12), channel_id=1, source_target_pairs={{1,0},{2,1},{3,2},{4,3},{5,4},{6,5},{7,6},{8,7},{9,8},{10,9},{11,1... | collective-permute-start | bytes 7864328 | tf_op jit(solution)/shard_map/ppermute | solution.py:18
  7.1 97.2 %collective-permute-start.2 = (bf16[8,320,320]{2,1,0:T(8,128)(2,1)}, bf16[8,320,320]{2,1,0:T(8,128)(2,1)}, u32[]{:S(2)}, u32[]{:S(2)}) collective-permute-start(bf16[8,320,320]{2,1,0:T(8,128)(2,1)} %param.16), channel_id=1, source_target_pairs={{0,1},{1,2},{2,3},{3,4},{4,5},{5,6},{6,7},{7,8},{8,9},{9,10},{10,1... | collective-permute-start | bytes 4915208 | tf_op jit(solution)/shard_map/ppermute | solution.py:17
  10.7 95.2 %collective-permute-start.3 = (bf16[8,320,320]{2,1,0:T(8,128)(2,1)}, bf16[8,320,320]{2,1,0:T(8,128)(2,1)}, u32[]{:S(2)}, u32[]{:S(2)}) collective-permute-start(bf16[8,320,320]{2,1,0:T(8,128)(2,1)} %param.16), channel_id=1, source_target_pairs={{1,0},{2,1},{3,2},{4,3},{5,4},{6,5},{7,6},{8,7},{9,8},{10,9},{11,1... | collective-permute-start | bytes 4915208 | tf_op jit(solution)/shard_map/ppermute | solution.py:18
  17.7 94.8 %copy-start.1 = (bf16[4,1024,320]{1,2,0:T(8,128)(2,1)S(1)}, bf16[4,1024,320]{1,2,0:T(8,128)(2,1)}, u32[]{:S(2)}) copy-start(bf16[4,1024,320]{1,2,0:T(8,128)(2,1)} %param.12) | copy-start | bytes 7864324
  118.2 11.6 %copy-start = (s32[256]{0:T(256)S(1)}, s32[256]{0:T(256)}, u32[]{:S(2)}) copy-start(s32[256]{0:T(256)} %param.17) | copy-start | bytes 3076
  324.0 0.5 copy-start.2
  439.3 24.4 %collective-permute-start.4 = (bf16[4,320,320]{2,0,1:T(4,128)(2,1)}, bf16[4,320,320]{2,0,1:T(4,128)(2,1)S(1)}, u32[]{:S(2)}, u32[]{:S(2)}) collective-permute-start(bf16[4,320,320]{2,0,1:T(4,128)(2,1)} %get-tuple-element.406), channel_id=1, source_target_pairs={{0,1},{1,2},{2,3},{3,4},{4,5},{5,6},{6,7},{7,8},{8,9},{9,10},{10,1... | collective-permute-start | bytes 2457608 | tf_op jit(solution)/shard_map/ppermute | solution.py:26
  441.9 22.8 %collective-permute-start.5 = (bf16[4,320,320]{2,0,1:T(4,128)(2,1)}, bf16[4,320,320]{2,0,1:T(4,128)(2,1)}, u32[]{:S(2)}, u32[]{:S(2)}) collective-permute-start(bf16[4,320,320]{2,0,1:T(4,128)(2,1)} %get-tuple-element.407), channel_id=1, source_target_pairs={{1,0},{2,1},{3,2},{4,3},{5,4},{6,5},{7,6},{8,7},{9,8},{10,9},{11,1... | collective-permute-start | bytes 2457608 | tf_op jit(solution)/shard_map/ppermute | solution.py:26
where the time goes:
time: 476 us; the launch traced here: 470 us
  local copies, waits for them, and re-layouts  175 us (37%)
  waiting for transfers between devices  106 us (22%)
  matrix products  79.3 us (17%)
  loops' own time  58 us (12%)
  other arithmetic  34.8 us (7%)
  starting transfers between devices  16.7 us (4%)
    dynamic_update_slice x24, local copies, waits for them, and re-layouts, local(): lax.map(one_pair, (local_ids, amplitudes, coupling_list, coupling_coef))  95.4 us
    ppermute x2, waiting for transfers between devices, with_halo(): before = lax.ppermute(last, axis, up)  86.5 us
    another operation x1, loops' own time, local(): lax.map(one_pair, (local_ids, amplitudes, coupling_list, coupling_coef))  57.9 us
    dot_general x8, matrix products, pair_terms(): lax.dot_general(left_block, aligned, (((0,), (0,)), ((), ())), preferred_...  30.9 us
    gather x8, local copies, waits for them, and re-layouts, one_pair(): near_amps = jnp.take(wide_amps, neighbours - pair_base, axis=0)  27.5 us
    dot_general x8, matrix products, left_density(): lax.dot_general(masked, masked, (((1,), (1,)), ((), ())), preferred_eleme...  18 us
    ppermute x2, waiting for transfers between devices, passed_along(): return lax.ppermute(block, axis, route)  18 us
    while x5, local copies, waits for them, and re-layouts, local(): lax.map(one_pair, (local_ids, amplitudes, coupling_list, coupling_coef))  15.2 us
  transfers between devices with their start and end apart: 6, of which 4 were waited for; matrix products, arithmetic and copies ran while one was open for 3% of the time, Pallas kernels for 0%

commit v1 on v0

v1 whole, which is shorter than its diff:
```python
import functools

import jax
import jax.numpy as jnp
from jax import lax
from jax.experimental import pallas as pl
from jax.experimental.pallas import tpu as pltpu
from jax.sharding import PartitionSpec as P

AXES = ("orb", "pair")
VMEM_BYTES = 48 * 1024 * 1024
NT = (((1,), (1,)), ((), ()))
TN = (((0,), (0,)), ((), ()))


def dot(a, b, dims=(((1,), (0,)), ((), ()))):
    return lax.dot_general(a, b, dims, preferred_element_type=jnp.float32)


def ones_where(equal):
    return jnp.where(equal, 1.0, 0.0).astype(jnp.bfloat16)


def live(rows, cols, shape):
    return (lax.broadcasted_iota(jnp.int32, shape, 0) < rows) & (
        lax.broadcasted_iota(jnp.int32, shape, 1) < cols
    )


def kept(amp, rows, cols):
    return jnp.where(live(rows, cols, amp.shape), amp.astype(jnp.float32), 0.0).astype(amp.dtype)


def projected(amp, left_col, left_row, right_col, right_row):
    rows = dot(ones_where(left_col == left_row), amp).astype(jnp.bfloat16)
    return dot(rows, ones_where(right_col == right_row), NT)


class Sizes:
    def __init__(self, blocks, amplitudes):
        self.occ = blocks.shape[0]
        self.aux = blocks.shape[1]
        self.pao = blocks.shape[2]
        self.pairs = amplitudes.shape[0]

    def first_orbital(self, pair):
        return pair // self.pairs * self.occ + lax.rem(pair, self.occ)


def own_kernel(
    s, ncpl, here, partner, listed, lens, coef, aux_rows, aux_col, pao_rows, left_col, right_col, blocks, amps, aligned, coupling, dens
):
    p = pl.program_id(0)
    me = here[0]
    left = lax.rem(p, s.occ)
    right = partner[me * s.pairs + p]

    @pl.when(p == 0)
    def _():
        dens[...] = jnp.zeros_like(dens)

    selector = ones_where(aux_col[left] == aux_rows[pl.ds(right, 1), :])
    aligned[0] = dot(blocks[left], selector).astype(jnp.bfloat16)

    coupling[...] = jnp.zeros_like(coupling)
    for c in range(ncpl):
        m = listed[p, c]
        spot = m - me * s.pairs

        @pl.when((spot >= 0) & (spot < s.pairs))
        def _():
            picked = projected(
                amps[spot],
                left_col[p],
                pao_rows[pl.ds(s.first_orbital(m), 1), :],
                right_col[p],
                pao_rows[pl.ds(partner[m], 1), :],
            )
            coupling[0] += coef[p, c] * picked

    masked = kept(amps[p], lens[me * s.occ + left], lens[right])
    dens[left] += dot(masked, masked, NT)
    near = right - me * s.occ

    @pl.when((near >= 0) & (near < s.occ))
    def _():
        dens[near] += dot(masked, masked, TN)


def near_kernel(
    s, ncpl, npair, here, partner, listed, lens, coef, pao_rows, left_col, right_col, before, after, part, dens_in, coupling, dens, wide
):
    p = pl.program_id(0)
    me = here[0]

    @pl.when(p == 0)
    def _():
        dens[...] = dens_in[...]
        for side, packed in enumerate((before, after)):
            for k in range(s.pairs):
                unpack(s, packed, k, wide.at[side * s.pairs + k])

    coupling[...] = part[...]
    for c in range(ncpl):
        m = listed[p, c]
        spot = m - me * s.pairs

        @pl.when((spot < 0) | (spot >= s.pairs))
        def _():
            picked = projected(
                wide[jnp.where(spot < 0, spot + s.pairs, spot)],
                left_col[p],
                pao_rows[pl.ds(s.first_orbital(m), 1), :],
                right_col[p],
                pao_rows[pl.ds(partner[m], 1), :],
            )
            coupling[0] += coef[p, c] * picked

    for side in range(2):
        m = (me + 2 * side - 1) * s.pairs + p
        inside = (m >= 0) & (m < npair)
        m = jnp.clip(m, 0, npair - 1)
        near = partner[m] - me * s.occ

        @pl.when(inside & (near >= 0) & (near < s.occ))
        def _():
            masked = kept(wide[side * s.pairs + p], lens[s.first_orbital(m)], lens[partner[m]])
            dens[near] += dot(masked, masked, TN)

    @pl.when(p == s.pairs - 1)
    def _():
        dens[...] = dens[...] / s.pao


def last_kernel(
    s, here, partner, lens, aligned, coupling, amps, gap_left, gap_right, before, own, after, new_amps, energy
):
    p = pl.program_id(0)
    me = here[0]
    right = partner[me * s.pairs + p]
    near = right - me * s.occ
    block = jnp.where(near < 0, before[0], jnp.where(near < s.occ, own[0], after[0]))
    mask = live(lens[me * s.occ + lax.rem(p, s.occ)], lens[right], (s.pao, s.pao))
    exchange = jnp.where(mask, dot(aligned[0], block, NT), 0.0)
    masked = jnp.where(mask, amps[0].astype(jnp.float32), 0.0)
    denom = gap_left[0] + gap_right[0]
    residual = exchange + denom * masked - coupling[0]
    new_amps[0] = (masked - 0.5 * residual / denom).astype(jnp.bfloat16)
    energy[p] = jnp.sum(exchange * masked) / s.pao


def packing(s):
    whole = s.pao // 128 * 128
    tail = s.pao - whole
    share = whole // tail
    return whole, tail, share


def pack(s, amps):
    whole, tail, share = packing(s)
    tails = amps[:, :, whole:]
    groups = s.pairs // share
    slots = [
        jnp.concatenate([tails[g * share + k] for k in range(share)], axis=-1) for g in range(groups)
    ]
    return jnp.concatenate([amps[:, :, :whole], jnp.stack(slots)], axis=0)


def unpack(s, packed, k, out):
    whole, tail, share = packing(s)
    out[:, :whole] = packed[k]
    spot = k % share * tail
    out[:, whole:] = packed[s.pairs + k // share, :, spot : spot + tail]


def along(array, distance):
    count = 1
    for axis in AXES:
        count *= lax.axis_size(axis)
    route = [(i - distance, i) for i in range(count) if 0 <= i - distance < count]
    return lax.ppermute(array, AXES, route)


def local(
    blocks, aux_domain, pao_domain, pao_gap, amplitudes, pair_partner, coupling_list, coupling_coef
):
    s = Sizes(blocks, amplitudes)
    ncpl = coupling_list.shape[1]
    npair = pair_partner.shape[0]
    me = lax.axis_index(AXES)
    here = me.astype(jnp.int32).reshape(1)
    blocks_t = jnp.swapaxes(blocks, 1, 2)
    packed = pack(s, amplitudes)
    amps_before = along(packed, 1)
    amps_after = along(packed, -1)
    blocks_before = along(blocks_t, 1)
    blocks_after = along(blocks_t, -1)

    own_ids = me * s.occ + jnp.arange(s.pairs, dtype=jnp.int32) % s.occ
    right_ids = lax.dynamic_slice_in_dim(pair_partner, me * s.pairs, s.pairs)
    lens = jnp.sum((pao_domain >= 0).astype(jnp.int32), axis=1)
    pao_cols = jnp.where(pao_domain < 0, -2, pao_domain)
    aux_col = lax.dynamic_slice_in_dim(aux_domain, me * s.occ, s.occ)[:, :, None]
    left_col = pao_cols[own_ids][:, :, None]
    right_col = pao_cols[right_ids][:, :, None]
    gap_left = pao_gap[own_ids][:, :, None]
    gap_right = pao_gap[right_ids][:, None, :]

    smem = pl.BlockSpec(memory_space=pltpu.SMEM)
    vmem = pl.BlockSpec(memory_space=pltpu.VMEM)
    params = pltpu.CompilerParams(
        dimension_semantics=("arbitrary",), vmem_limit_bytes=VMEM_BYTES
    )
    square = pl.BlockSpec((1, s.pao, s.pao), lambda p, *_: (p, 0, 0))
    all_dens = pl.BlockSpec((s.occ, s.pao, s.pao), lambda p, *_: (0, 0, 0))
    squares = jax.ShapeDtypeStruct((s.pairs, s.pao, s.pao), jnp.float32)
    dens_shape = jax.ShapeDtypeStruct((s.occ, s.pao, s.pao), jnp.float32)

    aligned, part, dens = pl.pallas_call(
        functools.partial(own_kernel, s, ncpl),
        grid=(s.pairs,),
        in_specs=[smem] * 5 + [vmem] * 7,
        out_specs=[pl.BlockSpec((1, s.pao, s.aux), lambda p: (p, 0, 0)), square, all_dens],
        out_shape=[
            jax.ShapeDtypeStruct((s.pairs, s.pao, s.aux), jnp.bfloat16),
            squares,
            dens_shape,
        ],
        compiler_params=params,
        cost_estimate=pl.CostEstimate(
            flops=2 * s.pairs * s.pao * s.aux * s.aux * 3, bytes_accessed=2 * 10**7, transcendentals=0
        ),
        name="own",
    )(
        here, pair_partner, coupling_list, lens, coupling_coef,
        aux_domain, aux_col, pao_domain, left_col, right_col, blocks_t, amplitudes,
    )

    coupling, densities = pl.pallas_call(
        functools.partial(near_kernel, s, ncpl, npair),
        grid=(s.pairs,),
        in_specs=[smem] * 5 + [vmem] * 5 + [square, all_dens],
        out_specs=[square, all_dens],
        out_shape=[squares, dens_shape],
        scratch_shapes=[pltpu.VMEM((2 * s.pairs, s.pao, s.pao), jnp.bfloat16)],
        compiler_params=params,
        cost_estimate=pl.CostEstimate(
            flops=2 * s.pairs * s.pao * s.aux * s.aux, bytes_accessed=2 * 10**7, transcendentals=0
        ),
        name="near",
    )(
        here, pair_partner, coupling_list, lens, coupling_coef,
        pao_domain, left_col, right_col, amps_before, amps_after, part, dens,
    )

    def block_spec(side):
        def index(p, here, partner, lens):
            near = partner[here[0] * s.pairs + p] - (here[0] + side) * s.occ
            return (jnp.clip(near, 0, s.occ - 1), 0, 0)

        return pl.BlockSpec((1, s.pao, s.aux), index)

    column = pl.BlockSpec((1, s.pao, 1), lambda p, *_: (p, 0, 0))
    row = pl.BlockSpec((1, 1, s.pao), lambda p, *_: (p, 0, 0))
    new_amps, energies = pl.pallas_call(
        functools.partial(last_kernel, s),
        grid_spec=pltpu.PrefetchScalarGridSpec(
            num_scalar_prefetch=3,
            grid=(s.pairs,),
            in_specs=[
                pl.BlockSpec((1, s.pao, s.aux), lambda p, *_: (p, 0, 0)),
                square,
                square,
                column,
                row,
                block_spec(-1),
                block_spec(0),
                block_spec(1),
            ],
            out_specs=[square, smem],
        ),
        out_shape=[
            jax.ShapeDtypeStruct(amplitudes.shape, amplitudes.dtype),
            jax.ShapeDtypeStruct((s.pairs,), jnp.float32),
        ],
        compiler_params=params,
        cost_estimate=pl.CostEstimate(
            flops=2 * s.pairs * s.pao * s.pao * s.aux, bytes_accessed=2 * 10**7, transcendentals=0
        ),
        name="last",
    )(
        here, pair_partner, lens,
        aligned, coupling, amplitudes, gap_left, gap_right, blocks_before, blocks_t, blocks_after,
    )
    return (new_amps, energies, densities)


def solution(mesh):
    return jax.shard_map(
        local,
        mesh=mesh,
        in_specs=(
            P(AXES, None, None),
            P(),
            P(),
            P(),
            P(AXES, None, None),
            P(),
            P(AXES, None),
            P(AXES, None),
        ),
        out_specs=(P(AXES, None, None), P(AXES), P(AXES, None, None)),
        check_vma=False,
    )
```

time: 476 us -> 116 us (0.24)
  local copies, waits for them, and re-layouts: 175 us -> 12 us
  matrix products: 79.3 us -> 0 us
  waiting for transfers between devices: 106 us -> 30.7 us
  loops' own time: 58 us -> 0 us
  Pallas kernels: 0 us -> 57.3 us
  other arithmetic: 34.8 us -> 1.81 us
    dynamic_update_slice x24 -> x0, local copies, waits for them, and re-layouts: 95.4 us -> none  [local(): lax.map(one_pair, (local_ids, amplitudes, coupling_list, coupling_coef))]
    dot_general x33 -> x0, matrix products: 79.3 us -> none  [the longest x8 30.9 us: pair_terms(): lax.dot_general(left_block, aligned, (((0,), (0,)), ((), ())), preferred_...]
    ppermute x6 -> x4, waiting for transfers between devices: 106 us -> 30.7 us  [along(): return lax.ppermute(array, AXES, route)]
    another operation x2 -> x0, loops' own time: 58 us -> none  [the longest x1 57.9 us: local(): lax.map(one_pair, (local_ids, amplitudes, coupling_list, coupling_coef))]
    pallas_call x0 -> x3, Pallas kernels: none -> 57.3 us  [the longest x1 26.6 us: local(): pl.pallas_call(functools.partial(own_kernel, s, ncpl), grid=(s.pairs,), i...]
    gather x33 -> x4, local copies, waits for them, and re-layouts: 42.9 us -> 2.26 us  [the longest x1 0.57 us: local(): gap_left = pao_gap[own_ids][:, :, None]]
    dynamic_slice x32 -> x0, local copies, waits for them, and re-layouts: 17.3 us -> none  [the longest x8 6.74 us: one_pair(): aux_domain[left]]
    reduce_sum x9 -> x0, other arithmetic: 17.2 us -> none  [the longest x8 14.5 us: pair_terms(): energy = jnp.sum(exchange * masked_f) / masked.shape[0]]
  transfers between devices with their start and end apart: 6 -> 4, of which waited for: 4 -> 3; matrix products, arithmetic and copies ran while one was open for 3% -> 6% of each run, Pallas kernels for 0% -> 39%
where the time goes in v1:
time: 116 us; the launch traced here: 115 us
  Pallas kernels  57.3 us (49%)
  waiting for transfers between devices  30.7 us (26%)
  starting transfers between devices  12.2 us (11%)
  local copies, waits for them, and re-layouts  12 us (10%)
  other arithmetic  1.81 us (2%)
    ppermute x4, waiting for transfers between devices, along(): return lax.ppermute(array, AXES, route)  30.7 us
    pallas_call x1, Pallas kernels, local(): pl.pallas_call(functools.partial(own_kernel, s, ncpl), grid=(s.pairs,), i...  26.6 us
    pallas_call x1, Pallas kernels, local(): pl.pallas_call(functools.partial(near_kernel, s, ncpl, npair), grid=(s.pa...  18.7 us
    ppermute x4, starting transfers between devices, along(): return lax.ppermute(array, AXES, route)  12.2 us
    pallas_call x1, Pallas kernels, local(): pl.pallas_call(functools.partial(last_kernel, s), grid_spec=pltpu.Prefetc...  12 us
    unnamed x22, local copies, waits for them, and re-layouts  3.03 us
  transfers between devices with their start and end apart: 4, of which 3 were waited for; matrix products, arithmetic and copies ran while one was open for 6% of the time, Pallas kernels for 39%

profile of v1, /device:TPU:1, one launch (start us, length us, event | category | flops | bytes accessed | tf_op | source)
XLA Modules:
  0.0 114.8 jit_solution(6207771535806591421)
XLA Ops:
  0.6 1.2 %slice_bitcast_fusion.7 = (bf16[320,64]{1,0:T(8,128)(2,1)S(1)}, bf16[320,64]{1,0:T(8,128)(2,1)S(1)}, bf16[320,64]{1,0:T(8,128)(2,1)S(1)}, bf16[320,64]{1,0:T(8,1...) fusion(bf16[8,320,320]{2,1,0:T(8,128)(2,1)} %amps.3), kind=kLoop, calls=%fused_computation.16 | loop fusion | bytes 655360 | tf_op jit(solution)/shard_map/squeeze | solution.py:164
  1.9 0.0 slice-start
  1.9 0.2 maximum_bitcast_fusion
  2.1 1.1 slice-done
  3.2 0.0 copy-start.2
  3.2 0.0 copy-start.5
  3.2 0.0 copy-start.6
  3.2 0.0 copy-start.7
  3.2 0.0 copy-start.8
  3.2 0.0 copy-start.3
  3.2 1.4 %pad_maximum_fusion = bf16[10,320,256]{2,1,0:T(8,128)(2,1)} fusion(bf16[1,320,256]{2,1,0:T(8,128)(2,1)S(1)} %get-tuple-element.28, bf16[1,320,256]{2,1,0:T(8,128)(2,1)S(1)} %get-tuple-element.27, bf16[8,320,256]{2,1,0:T(8,128)(2,1)S(1)} %slice-done), kind=kLoop, calls=%fused_computation.4 | loop fusion | flops 1638400 | bytes 3276800 | tf_op jit(solution)/shard_map/concatenate | solution.py:166
  4.6 4.5 %collective-permute-start = (bf16[10,320,256]{2,1,0:T(8,128)(2,1)}, bf16[10,320,256]{2,1,0:T(8,128)(2,1)}, u32[]{:S(2)}, u32[]{:S(2)}) collective-permute-start(bf16[10,320,256]{2,1,0:T(8,128)(2,1)} %pad_maximum_fusion), channel_id=1, source_target_pairs={{0,1},{1,2},{2,3},{3,4},{4,5},{5,6},{6,7},{7,8},{8,9},{9,10},{10,1... | collective-permute-start | bytes 4915208 | tf_op jit(solution)/shard_map/ppermute | solution.py:181
  9.1 1.9 %collective-permute-start.1 = (bf16[10,320,256]{2,1,0:T(8,128)(2,1)}, bf16[10,320,256]{2,1,0:T(8,128)(2,1)}, u32[]{:S(2)}, u32[]{:S(2)}) collective-permute-start(bf16[10,320,256]{2,1,0:T(8,128)(2,1)} %pad_maximum_fusion), channel_id=1, source_target_pairs={{1,0},{2,1},{3,2},{4,3},{5,4},{6,5},{7,6},{8,7},{9,8},{10,9},{11,1... | collective-permute-start | bytes 4915208 | tf_op jit(solution)/shard_map/ppermute | solution.py:181
  11.0 3.6 %collective-permute-start.2 = (bf16[4,320,1024]{2,1,0:T(8,128)(2,1)}, bf16[4,320,1024]{2,1,0:T(8,128)(2,1)}, u32[]{:S(2)}, u32[]{:S(2)}) collective-permute-start(bf16[4,320,1024]{2,1,0:T(8,128)(2,1)} %bitcast.5.blocks.own), channel_id=1, source_target_pairs={{0,1},{1,2},{2,3},{3,4},{4,5},{5,6},{6,7},{7,8},{8,9},{9,10},{10,1... | collective-permute-start | bytes 7864328 | tf_op jit(solution)/shard_map/ppermute | solution.py:181
  14.7 2.1 %collective-permute-start.3 = (bf16[4,320,1024]{2,1,0:T(8,128)(2,1)}, bf16[4,320,1024]{2,1,0:T(8,128)(2,1)}, u32[]{:S(2)}, u32[]{:S(2)}) collective-permute-start(bf16[4,320,1024]{2,1,0:T(8,128)(2,1)} %bitcast.5.blocks.own), channel_id=1, source_target_pairs={{1,0},{2,1},{3,2},{4,3},{5,4},{6,5},{7,6},{8,7},{9,8},{10,9},{11,1... | collective-permute-start | bytes 7864328 | tf_op jit(solution)/shard_map/ppermute | solution.py:181
  16.8 0.0 copy-done.2
  16.8 0.1 compare_select_fusion.1
  16.9 0.0 copy-done.5
  16.9 0.1 copy.22.pao_rows
  17.1 0.1 compare_select_fusion
  17.2 0.6 gather_fusion
  17.8 0.6 gather_fusion.1
  18.3 0.0 copy-done.6
  18.3 0.1 copy.36
  18.5 0.6 gather_fusion.2
  19.0 0.6 gather_fusion.3
  19.6 0.0 copy-done.7
  19.6 0.1 copy.25.listed
  19.7 0.0 copy-done.8
  19.7 0.1 copy.26.coef
  19.8 0.0 copy-done.3
  19.8 2.0 %copy.27.aux_col = s32[4,1024,1]{2,1,0:T(8,128)} copy(s32[4,1024,1]{1,0,2:T(4,128)S(1)} %dynamic-slice_bitcast_fusion) | data formatting | bytes 32768 | tf_op jit(solution)/shard_map/broadcast_in_dim | solution.py:203
  21.8 0.4 copy.29.left_col
  22.2 1.5 %copy.30.right_col = s32[8,320,1]{2,1,0:T(8,128)} copy(s32[8,320,1]{1,0,2:T(8,128)S(1)} %bitcast.29) | data formatting | bytes 20480 | tf_op jit(solution)/shard_map/broadcast_in_dim | solution.py:205
  23.7 0.4 copy.38.gap_left
  24.2 0.0 copy-start.1
  24.2 1.3 %copy-done.1 = s32[8,320,1]{2,1,0:T(8,128)S(1)} copy-done((s32[8,320,1]{2,1,0:T(8,128)S(1)}, s32[8,320,1]{2,1,0:T(8,128)}, u32[]{:S(2)}) %copy-start.1) | copy-done | bytes 10264
  25.5 26.6 %own.1 = (bf16[8,320,1024]{2,1,0:T(8,128)(2,1)}, f32[8,320,320]{2,1,0:T(8,128)}, f32[4,320,320]{2,1,0:T(8,128)S(1)}) custom-call(s32[1]{0:T(128)} %bitcast.here, s32[256]{0:T(256)S(1)} %copy-done.2, s32[8,4]{1,0:T(8,128)S(1)} %copy.25.listed, s32[128]{0:T(128)S(1)} %get-tuple-element.26.lens, f32[8,4]{1,0:T(8,128)S(1)} %copy.26.coef, ...), custom_call_target="tpu_custom_call" | custom-call | flops 16106127360 | bytes 20000000 | tf_op jit(solution)/shard_map/own/pallas_call | solution.py:219
  52.1 0.0 copy-start.4
  52.1 1.3 %copy-done.4 = f32[4,320,320]{2,1,0:T(8,128)} copy-done((f32[4,320,320]{2,1,0:T(8,128)}, f32[4,320,320]{2,1,0:T(8,128)S(1)}, u32[]{:S(2)}) %copy-start.4) | copy-done | bytes 1638424
  53.4 19.7 %collective-permute-done.before = bf16[10,320,256]{2,1,0:T(8,128)(2,1)} collective-permute-done((bf16[10,320,256]{2,1,0:T(8,128)(2,1)}, bf16[10,320,256]{2,1,0:T(8,128)(2,1)}, u32[]{:S(2)}, u32[]{:S(2)}) %collective-permute-start) | collective-permute-done | bytes 1638432 | tf_op jit(solution)/shard_map/ppermute | solution.py:181
  73.1 0.0 collective-permute-done.1.after
  73.1 0.0 copy-start
  73.1 18.7 %near.1 = (f32[8,320,320]{2,1,0:T(8,128)}, f32[4,320,320]{2,1,0:T(8,128)}) custom-call(s32[1]{0:T(128)} %bitcast.here, s32[256]{0:T(256)S(1)} %copy-done.2, s32[8,4]{1,0:T(8,128)S(1)} %copy.25.listed, s32[128]{0:T(128)S(1)} %get-tuple-element.26.lens, f32[8,4]{1,0:T(8,128)S(1)} %copy.26.coef, s32[128,320]{1,0:T(8,128)S(1)} %copy.22.pao_rows, ...), custom_call_target="tpu_custom_call" | custom-call | flops 5368709120 | bytes 20000000 | tf_op jit(solution)/shard_map/near/pallas_call | solution.py:239
  91.8 9.4 %collective-permute-done.2.before = bf16[4,320,1024]{2,1,0:T(8,128)(2,1)} collective-permute-done((bf16[4,320,1024]{2,1,0:T(8,128)(2,1)}, bf16[4,320,1024]{2,1,0:T(8,128)(2,1)}, u32[]{:S(2)}, u32[]{:S(2)}) %collective-permute-start.2) | collective-permute-done | bytes 2621472 | tf_op jit(solution)/shard_map/ppermute | solution.py:181
  101.2 1.6 %collective-permute-done.3.after = bf16[4,320,1024]{2,1,0:T(8,128)(2,1)} collective-permute-done((bf16[4,320,1024]{2,1,0:T(8,128)(2,1)}, bf16[4,320,1024]{2,1,0:T(8,128)(2,1)}, u32[]{:S(2)}, u32[]{:S(2)}) %collective-permute-start.3) | collective-permute-done | bytes 2621472 | tf_op jit(solution)/shard_map/ppermute | solution.py:181
  102.8 0.0 copy-done
  102.8 12.0 %last.1 = (bf16[8,320,320]{2,1,0:T(8,128)(2,1)}, f32[8]{0:T(128)}) custom-call(s32[1]{0:T(128)} %bitcast.here, s32[256]{0:T(256)S(1)} %copy-done.2, s32[128]{0:T(128)S(1)} %get-tuple-element.26.lens, bf16[8,320,1024]{2,1,0:T(8,128)(2,1)} %get-tuple-element.10.aligned, f32[8,320,320]{2,1,0:T(8,128)} %get-tuple-element.13.coupling, ...), custom_call_target="tpu_custom_call" | custom-call | flops 1677721600 | bytes 20000000 | tf_op jit(solution)/shard_map/last/pallas_call | solution.py:265
  (5 shorter events, 0.0 us)
Async XLA Ops:
  1.9 1.3 %slice-start = ((bf16[8,320,320]{2,1,0:T(8,128)(2,1)}), bf16[8,320,256]{2,1,0:T(8,128)(2,1)S(1)}, s32[]{:S(2)}) async-start(bf16[8,320,320]{2,1,0:T(8,128)(2,1)} %amps.3), calls=%async_computation | async-start | bytes 2621440 | tf_op jit(solution)/shard_map/slice | solution.py:166
  3.2 13.7 %copy-start.2 = (s32[256]{0:T(256)S(1)}, s32[256]{0:T(256)}, u32[]{:S(2)}) copy-start(s32[256]{0:T(256)} %partner.5) | copy-start | bytes 3076
  3.2 13.8 %copy-start.5 = (s32[128,320]{0,1:T(8,128)S(1)}, s32[128,320]{0,1:T(8,128)}, u32[]{:S(2)}) copy-start(s32[128,320]{0,1:T(8,128)} %param.10) | copy-start | bytes 491524
  3.2 15.2 %copy-start.6 = (f32[128,320]{0,1:T(8,128)S(1)}, f32[128,320]{0,1:T(8,128)}, u32[]{:S(2)}) copy-start(f32[128,320]{0,1:T(8,128)} %param.11) | copy-start | bytes 491524
  3.2 16.4 %copy-start.7 = (s32[8,4]{0,1:T(4,128)S(1)}, s32[8,4]{0,1:T(4,128)}, u32[]{:S(2)}) copy-start(s32[8,4]{0,1:T(4,128)} %param.14) | copy-start | bytes 388
  3.2 16.5 %copy-start.8 = (f32[8,4]{0,1:T(4,128)S(1)}, f32[8,4]{0,1:T(4,128)}, u32[]{:S(2)}) copy-start(f32[8,4]{0,1:T(4,128)} %param.15) | copy-start | bytes 388
  3.2 16.6 %copy-start.3 = (s32[128,1024]{1,0:T(8,128)S(1)}, s32[128,1024]{1,0:T(8,128)}, u32[]{:S(2)}) copy-start(s32[128,1024]{1,0:T(8,128)} %aux_rows.1) | copy-start | bytes 1572868
  4.6 68.5 %collective-permute-start = (bf16[10,320,256]{2,1,0:T(8,128)(2,1)}, bf16[10,320,256]{2,1,0:T(8,128)(2,1)}, u32[]{:S(2)}, u32[]{:S(2)}) collective-permute-start(bf16[10,320,256]{2,1,0:T(8,128)(2,1)} %pad_maximum_fusion), channel_id=1, source_target_pairs={{0,1},{1,2},{2,3},{3,4},{4,5},{5,6},{6,7},{7,8},{8,9},{9,10},{10,1... | collective-permute-start | bytes 4915208 | tf_op jit(solution)/shard_map/ppermute | solution.py:181
  9.1 64.0 %collective-permute-start.1 = (bf16[10,320,256]{2,1,0:T(8,128)(2,1)}, bf16[10,320,256]{2,1,0:T(8,128)(2,1)}, u32[]{:S(2)}, u32[]{:S(2)}) collective-permute-start(bf16[10,320,256]{2,1,0:T(8,128)(2,1)} %pad_maximum_fusion), channel_id=1, source_target_pairs={{1,0},{2,1},{3,2},{4,3},{5,4},{6,5},{7,6},{8,7},{9,8},{10,9},{11,1... | collective-permute-start | bytes 4915208 | tf_op jit(solution)/shard_map/ppermute | solution.py:181
  11.0 90.2 %collective-permute-start.2 = (bf16[4,320,1024]{2,1,0:T(8,128)(2,1)}, bf16[4,320,1024]{2,1,0:T(8,128)(2,1)}, u32[]{:S(2)}, u32[]{:S(2)}) collective-permute-start(bf16[4,320,1024]{2,1,0:T(8,128)(2,1)} %bitcast.5.blocks.own), channel_id=1, source_target_pairs={{0,1},{1,2},{2,3},{3,4},{4,5},{5,6},{6,7},{7,8},{8,9},{9,10},{10,1... | collective-permute-start | bytes 7864328 | tf_op jit(solution)/shard_map/ppermute | solution.py:181
  14.7 88.2 %collective-permute-start.3 = (bf16[4,320,1024]{2,1,0:T(8,128)(2,1)}, bf16[4,320,1024]{2,1,0:T(8,128)(2,1)}, u32[]{:S(2)}, u32[]{:S(2)}) collective-permute-start(bf16[4,320,1024]{2,1,0:T(8,128)(2,1)} %bitcast.5.blocks.own), channel_id=1, source_target_pairs={{1,0},{2,1},{3,2},{4,3},{5,4},{6,5},{7,6},{8,7},{9,8},{10,9},{11,1... | collective-permute-start | bytes 7864328 | tf_op jit(solution)/shard_map/ppermute | solution.py:181
  24.2 1.3 %copy-start.1 = (s32[8,320,1]{2,1,0:T(8,128)S(1)}, s32[8,320,1]{2,1,0:T(8,128)}, u32[]{:S(2)}) copy-start(s32[8,320,1]{2,1,0:T(8,128)} %copy.30.right_col) | copy-start | bytes 30724
  52.1 1.3 %copy-start.4 = (f32[4,320,320]{2,1,0:T(8,128)}, f32[4,320,320]{2,1,0:T(8,128)S(1)}, u32[]{:S(2)}) copy-start(f32[4,320,320]{2,1,0:T(8,128)S(1)} %get-tuple-element.12.dens_in) | copy-start | bytes 4915204
  73.1 29.7 %copy-start = (bf16[8,320,320]{2,1,0:T(8,128)(2,1)S(1)}, bf16[8,320,320]{2,1,0:T(8,128)(2,1)}, u32[]{:S(2)}) copy-start(bf16[8,320,320]{2,1,0:T(8,128)(2,1)} %amps.3) | copy-start | bytes 4915204

commit v2 on v1

v2 whole, which is shorter than its diff:
```python
import functools

import jax
import jax.numpy as jnp
from jax import lax
from jax.experimental import pallas as pl
from jax.experimental.pallas import tpu as pltpu
from jax.sharding import PartitionSpec as P

AXES = ("orb", "pair")
VMEM_BYTES = 48 * 1024 * 1024
AUX_IDS = 2048
LOW = 64
HIGH = AUX_IDS // LOW
BASE = 32
LANES = 128
FIRST, WHOLE = 18, 32
NN = (((1,), (0,)), ((), ()))
NT = (((1,), (1,)), ((), ()))
TN = (((0,), (0,)), ((), ()))


def dot(a, b, dims=NN):
    return lax.dot_general(a, b, dims, preferred_element_type=jnp.float32)


def one_where(equal, value=1.0):
    return jnp.where(equal, value, 0.0).astype(jnp.bfloat16)


def iota(shape, dim):
    return lax.broadcasted_iota(jnp.int32, shape, dim)


def live(rows, cols, shape):
    return (iota(shape, 0) < rows) & (iota(shape, 1) < cols)


def kept(amp, rows, cols):
    return jnp.where(live(rows, cols, amp.shape), amp.astype(jnp.float32), 0.0).astype(amp.dtype)


def column(row):
    return jnp.broadcast_to(row, (LANES, row.shape[1])).T


def same(col, row):
    parts = []
    for at in range(0, row.shape[1], LANES):
        piece = row[:, at : at + LANES]
        parts.append(one_where(col[:, : piece.shape[1]] == piece))
    return jnp.concatenate(parts, axis=1)


def chunks_of(count):
    return (count + LANES - 1) // LANES


def rows_of(length):
    return (length + 15) // 16 * 16


def swapped(me):
    odd = lax.rem(me, 2)
    return me + 1 - 2 * odd, me - 1 + 2 * odd


class Sizes:
    def __init__(self, blocks, amplitudes, pair_partner):
        self.occ = blocks.shape[0]
        self.aux = blocks.shape[1]
        self.pao = blocks.shape[2]
        self.pairs = amplitudes.shape[0]
        self.npair = pair_partner.shape[0]
        self.nocc = self.npair // self.pairs * self.occ
        self.rows = self.occ * self.pao * (self.aux // LANES)
        self.first = self.rows * FIRST // WHOLE // 16 * 16

    def first_orbital(self, pair):
        return pair // self.pairs * self.occ + lax.rem(pair, self.occ)

    def where_partner(self, me, right):
        device = right // self.occ
        sibling, _ = swapped(me)
        kind = jnp.where(device == me, 2, jnp.where(device == sibling, 0, 1))
        return kind * self.occ + lax.rem(right, self.occ), kind


def packing(s):
    whole = s.pao // LANES * LANES
    tail = s.pao - whole
    share = whole // tail
    return whole, tail, share


def slim_kernel(s, amps, out):
    whole, tail, share = packing(s)
    for k in range(s.pairs):
        out[k] = amps[k, :, :whole]
    for g in range(s.pairs // share):
        tails = [amps[g * share + t, :, whole:] for t in range(share)]
        out[s.pairs + g] = jnp.concatenate(tails, axis=1)


def unpack(s, packed, k, out):
    whole, tail, share = packing(s)
    out[:, :whole] = packed[k]
    spot = k % share * tail
    out[:, whole:] = packed[s.pairs + k // share, :, spot : spot + tail]


def places(high, weight, table):
    found = dot(high[:, :HIGH], table).astype(jnp.bfloat16) * weight
    return dot(found, jnp.ones((LANES, LANES), jnp.bfloat16))


def picker(place, chunk):
    spot = iota(place.shape, 1).astype(jnp.float32) + (chunk * LANES + 1).astype(jnp.float32)
    return jnp.concatenate([one_where(place == spot), one_where(place == spot + LANES)], axis=1)


def split_place(place, lane):
    part = jnp.where(lane < LOW, place // BASE, lax.rem(place, BASE))
    return part.astype(jnp.float32)


def pack_kernel(
    s, here, partner, lens, aux_rows, blocks, to_sibling, to_other, to_other_more, high, weight, tables, counts, offsets, load, maps, sends, bufs, sems
):
    me = here[0]
    peers = swapped(me)

    for g, device in enumerate((me,) + peers):
        for k in range(s.occ):
            orbital = jnp.clip(device * s.occ + k, 0, s.nocc - 1)
            row = aux_rows[pl.ds(orbital, 1), :]
            lane = iota((LANES, s.aux), 0)
            matches = lax.rem(lane, LOW) == lax.rem(row, LOW)
            by_high = one_where(iota((HIGH, s.aux), 0) == row // LOW)
            maps[g * s.occ + k] = dot(by_high, one_where(matches), NT)
            if g == 0:
                spot = split_place(iota((LANES, s.aux), 1) + 1, lane)
                table = dot(by_high, one_where(matches, spot), NT)
                tables[2 * s.occ + k] = table.astype(jnp.bfloat16)
                col = column(row)
                lane = iota((s.aux, LANES), 1)
                high[k] = one_where(col // LOW == lane)
                weight[k] = one_where(
                    lax.rem(col, LOW) == lax.rem(lane, LOW), jnp.where(lane < LOW, 1.0 * BASE, 1.0)
                )

    lane_in, lane_out = iota((LANES, LANES), 0), iota((LANES, LANES), 1)
    ahead = one_where((lane_in < LOW) & (lane_in < lax.rem(lane_out, LOW)))
    first = one_where(lane_in < LOW)
    above = one_where(iota((HIGH, HIGH), 1) < iota((HIGH, HIGH), 0))
    lane = iota((HIGH, LANES), 1)

    def listing(target, users, device, orbital):
        union = jnp.zeros((HIGH, LANES), jnp.float32)
        for q in range(s.pairs):
            pair = device * s.pairs + q
            inside = (pair >= 0) & (pair < s.npair)
            uses = inside & (partner[jnp.clip(pair, 0, s.npair - 1)] == orbital)
            union += jnp.where(uses, 1.0, 0.0) * maps[users + q % s.occ]
        taken = (union > 0.0) & (maps[target] > 0.0)
        flags = one_where(taken)
        total = dot(flags, first)
        place = dot(flags, ahead) + dot(above, total.astype(jnp.bfloat16)) + 1.0
        place = jnp.where(taken, place, 0.0).astype(jnp.int32)
        count = jnp.sum(jnp.where(lane == 0, total, 0.0)).astype(jnp.int32)
        return split_place(place, lane).astype(jnp.bfloat16), count

    for r in range(2):
        at, load[r] = jnp.int32(0), jnp.int32(0)
        for k in range(s.occ):
            l = r * s.occ + k
            orbital = jnp.clip(peers[r] * s.occ + k, 0, s.nocc - 1)
            tables[l], counts[l] = listing((1 + r) * s.occ + k, 0, me, peers[r] * s.occ + k)
            offsets[l] = at
            at += chunks_of(counts[l]) * rows_of(lens[orbital])
    for k in range(s.occ):
        counts[2 * s.occ + k] = jnp.int32(s.aux)
        offsets[2 * s.occ + k] = jnp.int32(0)

    copies = []
    for r in (1, 0):
        at = jnp.int32(0)
        for k in range(s.occ):
            table, count = listing(k, (1 + r) * s.occ, peers[r], me * s.occ + k)
            sends[k] = table
            step = rows_of(lens[me * s.occ + k])

            @pl.when(count > 0)
            def _(k=k, at=at, step=step, count=count):
                place = places(high[k], weight[k], sends[k])

                def some(c, _):
                    got = dot(blocks[k], picker(place, 2 * c)).astype(jnp.bfloat16)
                    spot = pl.multiple_of(at + 2 * c * step, 16)
                    bufs[r, pl.ds(spot, s.pao), :] = got[:, :LANES]

                    @pl.when((2 * c + 1) * LANES < count)
                    def _():
                        bufs[r, pl.ds(pl.multiple_of(spot + step, 16), s.pao), :] = got[:, LANES:]

                    return 0

                lax.fori_loop(0, (chunks_of(count) + 1) // 2, some, 0)

            at += chunks_of(count) * step
        load[r] = at
        if r == 1:
            copies = [
                pltpu.make_async_copy(bufs.at[1, pl.ds(0, s.first)], to_other, sems.at[0]),
                pltpu.make_async_copy(
                    bufs.at[1, pl.ds(s.first, s.rows - s.first)], to_other_more, sems.at[1]
                ),
            ]
        else:
            copies = [pltpu.make_async_copy(bufs.at[0, pl.ds(0, s.rows)], to_sibling, sems.at[2])]
        for copy in copies:
            copy.start()
        if r == 1:
            pending = copies
    for copy in pending + copies:
        copy.wait()


def own_kernel(s, here, partner, lens, counts, tables, blocks, high, weight, amps, aligned, dens):
    g = pl.program_id(0)
    me = here[0]
    left, p = paired(s, g)
    right = partner[me * s.pairs + p]
    wide = 2 * LANES
    l, _ = s.where_partner(me, right)
    place = places(high[0], weight[0], tables[l])

    def some(c, _):
        at = pl.multiple_of(c * wide, wide)
        aligned[0, :, pl.ds(at, wide)] = dot(blocks[0], picker(place, 2 * c)).astype(jnp.bfloat16)
        return 0

    lax.fori_loop(0, (chunks_of(counts[l]) + 1) // 2, some, 0)

    masked = kept(amps[0], lens[me * s.occ + left], lens[right])
    term = dot(masked, masked, NT)

    @pl.when(lax.rem(g, s.pairs // s.occ) == 0)
    def _():
        dens[0] = term

    @pl.when(lax.rem(g, s.pairs // s.occ) != 0)
    def _():
        dens[0] += term


def paired(s, g):
    repeats = s.pairs // s.occ
    left = g // repeats
    return left, lax.rem(g, repeats) * s.occ + left


def near_kernel(
    s, ncpl, here, partner, listed, lens, coef, pao_rows, sibling, own, other, dens_in, coupling, dens, wide, tall, dens_own, sem
):
    p = pl.program_id(0)
    me = here[0]
    peers = swapped(me)
    fetch = pltpu.make_async_copy(dens_in, dens_own, sem)

    @pl.when(p == 0)
    def _():
        fetch.start()
        dens[...] = jnp.zeros_like(dens)
        wide[s.pairs : 2 * s.pairs] = own[...]
        for device, packed in zip(peers, (sibling, other)):
            for k in range(s.pairs):
                unpack(s, packed, k, wide.at[(device - me + 1) * s.pairs + k])

    def row_of(orbital):
        return pao_rows[pl.ds(orbital, 1), :]

    def column_of(orbital):
        row = row_of(orbital)
        return column(jnp.where(row < 0, -2, row))

    right_col = column_of(partner[me * s.pairs + p])
    left_col = column_of(me * s.occ + lax.rem(p, s.occ))
    left_rows = []
    for c in range(ncpl):
        m = listed[p, c]
        left_rows.append(row_of(s.first_orbital(m)))
        amp = wide[m - (me - 1) * s.pairs]
        moved = dot(amp, same(right_col, row_of(partner[m])), NT)
        tall[c * s.pao : (c + 1) * s.pao] = (coef[p, c] * moved).astype(jnp.bfloat16)
    coupling[0] = dot(same(left_col, jnp.concatenate(left_rows, axis=1)), tall[...])

    for side in range(3):
        m = (me + side - 1) * s.pairs + p
        inside = (m >= 0) & (m < s.npair)
        m = jnp.clip(m, 0, s.npair - 1)
        near = partner[m] - me * s.occ

        @pl.when(inside & (near >= 0) & (near < s.occ))
        def _():
            amp = wide[side * s.pairs + p]
            masked = kept(amp, lens[s.first_orbital(m)], lens[partner[m]])
            dens[near] += dot(masked, masked, TN)

    @pl.when(p == s.pairs - 1)
    def _():
        fetch.wait()
        dens[...] = (dens[...] + dens_own[...]) / s.pao


def update(s, lens_left, lens_right, exchange, amp, coupling, gap_left, gap_right):
    mask = live(lens_left, lens_right, (s.pao, s.pao))
    exchange = jnp.where(mask, exchange, 0.0)
    masked = jnp.where(mask, amp.astype(jnp.float32), 0.0)
    left = column(gap_left)
    parts = []
    for at in range(0, s.pao, LANES):
        lanes = slice(at, min(at + LANES, s.pao))
        part = masked[:, lanes]
        denom = left[:, : part.shape[1]] + gap_right[:, lanes]
        residual = exchange[:, lanes] + denom * part - coupling[:, lanes]
        parts.append((part - 0.5 * residual / denom).astype(jnp.bfloat16))
    return jnp.concatenate(parts, axis=1), jnp.sum(exchange * masked) / s.pao


def compacted(s, count, at, step, aligned, halo, sums):
    sums[...] = jnp.zeros_like(sums)
    wide = 2 * LANES

    def some(c, _):
        spot = pl.multiple_of(at + 2 * c * step, 16)
        one = halo[pl.ds(spot, s.pao), :]
        two = halo[pl.ds(pl.multiple_of(spot + step, 16), s.pao), :]
        two = jnp.where((2 * c + 1) * LANES < count, two, jnp.zeros_like(two))
        lanes = pl.ds(pl.multiple_of(c * wide, wide), wide)
        sums[...] += dot(aligned[:, lanes], jnp.concatenate([one, two], axis=1), NT)
        return 0

    lax.fori_loop(0, (chunks_of(count) + 1) // 2, some, 0)


def mid_kernel(
    s, here, partner, lens, counts, offsets, gaps, aligned, coupling, amps, own, sibling, new_amps, energy, halo, sums, sem
):
    p = pl.program_id(0)
    me = here[0]
    left, right = me * s.occ + lax.rem(p, s.occ), partner[me * s.pairs + p]
    l, kind = s.where_partner(me, right)

    @pl.when(p == 0)
    def _():
        copy = pltpu.make_async_copy(sibling, halo.at[pl.ds(0, s.rows), :], sem)
        copy.start()
        copy.wait()

    @pl.when(kind == 2)
    def _():
        sums[...] = dot(aligned[0], own[lax.rem(right, s.occ)], NT)

    @pl.when(kind == 0)
    def _():
        compacted(s, counts[l], offsets[l], rows_of(lens[right]), aligned.at[0], halo, sums)

    @pl.when(kind != 1)
    def _():
        new_amps[0], energy[p] = update(
            s, lens[left], lens[right], sums[...], amps[0], coupling[0], gaps[pl.ds(left, 1), :], gaps[pl.ds(right, 1), :]
        )

    @pl.when(kind == 1)
    def _():
        new_amps[0] = jnp.zeros_like(amps[0])
        energy[p] = 0.0


def last_kernel(
    s, here, partner, lens, counts, offsets, over, energy_in, gaps, aligned, coupling, amps, other, more, _, new_amps, energy, halo, held, terms, olds, news, sums, sems
):
    me = here[0]

    def copies(p):
        return [
            pltpu.make_async_copy(aligned.at[p], held.at[p], sems.at[0, p]),
            pltpu.make_async_copy(coupling.at[p], terms.at[p], sems.at[1, p]),
            pltpu.make_async_copy(amps.at[p], olds.at[p], sems.at[2, p]),
        ]

    def result(p):
        return pltpu.make_async_copy(news.at[p], new_amps.at[p], sems.at[3, p])

    def each(act):
        def one(p, _):
            right = partner[me * s.pairs + p]
            l, kind = s.where_partner(me, right)

            @pl.when(kind == 1)
            def _():
                act(p, right, l)

            return 0

        lax.fori_loop(0, s.pairs, one, 0)

    first = pltpu.make_async_copy(other, halo.at[pl.ds(0, s.first)], sems.at[4, 0])
    rest = pltpu.make_async_copy(more, halo.at[pl.ds(s.first, s.rows - s.first)], sems.at[4, 1])
    first.start()

    @pl.when(over[0] > 0)
    def _():
        rest.start()
        rest.wait()

    def begin(p, right, l):
        for copy in copies(p):
            copy.start()

    def finish(p, right, l):
        left = me * s.occ + lax.rem(p, s.occ)
        for copy in copies(p):
            copy.wait()
        compacted(s, counts[l], offsets[l], rows_of(lens[right]), held.at[p], halo, sums)
        news[p], energy[p] = update(
            s, lens[left], lens[right], sums[...], olds[p], terms[p], gaps[pl.ds(left, 1), :], gaps[pl.ds(right, 1), :]
        )
        result(p).start()

    for p in range(s.pairs):
        energy[p] = energy_in[p]
    each(begin)
    first.wait()
    each(finish)
    each(lambda p, right, l: result(p).wait())


def swap(array, role):
    count = 1
    for axis in AXES:
        count *= lax.axis_size(axis)
    route = []
    for low in range(role, count - 1, 2):
        route += [(low, low + 1), (low + 1, low)]
    return lax.ppermute(array, AXES, route)


def local(
    blocks, aux_domain, pao_domain, pao_gap, amplitudes, pair_partner, coupling_list, coupling_coef
):
    s = Sizes(blocks, amplitudes, pair_partner)
    ncpl = coupling_list.shape[1]
    me = lax.axis_index(AXES)
    here = me.astype(jnp.int32).reshape(1)
    blocks_t = jnp.swapaxes(blocks, 1, 2)

    smem = pl.BlockSpec(memory_space=pltpu.SMEM)
    vmem = pl.BlockSpec(memory_space=pltpu.VMEM)
    anywhere = pl.BlockSpec(memory_space=pl.ANY)
    plain = pltpu.CompilerParams(vmem_limit_bytes=VMEM_BYTES)
    stepped = pltpu.CompilerParams(
        dimension_semantics=("arbitrary",), vmem_limit_bytes=VMEM_BYTES
    )
    square = pl.BlockSpec((1, s.pao, s.pao), lambda p, *_: (p, 0, 0))
    all_dens = pl.BlockSpec((s.occ, s.pao, s.pao), lambda p, *_: (0, 0, 0))
    squares = jax.ShapeDtypeStruct((s.pairs, s.pao, s.pao), jnp.float32)
    dens_shape = jax.ShapeDtypeStruct((s.occ, s.pao, s.pao), jnp.float32)

    def cost(work, data):
        return pl.CostEstimate(flops=work, bytes_accessed=data, transcendentals=0)

    whole, tail, share = packing(s)
    slim = pl.pallas_call(
        functools.partial(slim_kernel, s),
        in_specs=[vmem],
        out_specs=vmem,
        out_shape=jax.ShapeDtypeStruct((s.pairs + s.pairs // share, s.pao, whole), jnp.bfloat16),
        compiler_params=plain,
        cost_estimate=cost(10**6, 4 * 10**6),
        name="slim",
    )(amplitudes)
    amps_other = swap(slim, 1)
    amps_sibling = swap(slim, 0)

    lens = jnp.sum((pao_domain >= 0).astype(jnp.int32), axis=1)

    tables_number = 3 * s.occ
    to_sibling, to_other, to_other_more, high, weight, tables, counts, offsets, load = pl.pallas_call(
        functools.partial(pack_kernel, s),
        in_specs=[smem] * 3 + [vmem] * 2,
        out_specs=[anywhere] * 3 + [vmem] * 3 + [smem] * 3,
        out_shape=[
            jax.ShapeDtypeStruct((s.rows, LANES), jnp.bfloat16),
            jax.ShapeDtypeStruct((s.first, LANES), jnp.bfloat16),
            jax.ShapeDtypeStruct((s.rows - s.first, LANES), jnp.bfloat16),
            jax.ShapeDtypeStruct((s.occ, s.aux, LANES), jnp.bfloat16),
            jax.ShapeDtypeStruct((s.occ, s.aux, LANES), jnp.bfloat16),
            jax.ShapeDtypeStruct((tables_number, HIGH, LANES), jnp.bfloat16),
            jax.ShapeDtypeStruct((tables_number,), jnp.int32),
            jax.ShapeDtypeStruct((tables_number,), jnp.int32),
            jax.ShapeDtypeStruct((2,), jnp.int32),
        ],
        scratch_shapes=[
            pltpu.VMEM((3 * s.occ, HIGH, LANES), jnp.float32),
            pltpu.VMEM((s.occ, HIGH, LANES), jnp.bfloat16),
            pltpu.VMEM((2, s.rows + s.pao, LANES), jnp.bfloat16),
            pltpu.SemaphoreType.DMA((3,)),
        ],
        compiler_params=plain,
        cost_estimate=cost(2 * 10**9, 10**7),
        name="pack",
    )(here, pair_partner, lens, aux_domain, blocks_t)

    from_other = swap(to_other, 1)
    from_sibling = swap(to_sibling, 0)
    loads = lax.all_gather(load[1:], AXES, tiled=True)
    over = jnp.max(loads) > s.first

    def by_left(block, *rest):
        return pl.BlockSpec((1,) + block, lambda g: (paired(s, g)[0], 0, 0))

    aligned, dens = pl.pallas_call(
        functools.partial(own_kernel, s),
        grid=(s.pairs,),
        in_specs=[smem] * 4
        + [
            vmem,
            by_left((s.pao, s.aux)),
            by_left((s.aux, LANES)),
            by_left((s.aux, LANES)),
            pl.BlockSpec((1, s.pao, s.pao), lambda g: (paired(s, g)[1], 0, 0)),
        ],
        out_specs=[
            pl.BlockSpec((1, s.pao, s.aux), lambda g: (paired(s, g)[1], 0, 0)),
            by_left((s.pao, s.pao)),
        ],
        out_shape=[
            jax.ShapeDtypeStruct((s.pairs, s.pao, s.aux), jnp.bfloat16),
            dens_shape,
        ],
        compiler_params=stepped,
        cost_estimate=cost(2 * s.pairs * s.pao * s.aux * s.aux * 2, 2 * 10**7),
        name="own",
    )(here, pair_partner, lens, counts, tables, blocks_t, high, weight, amplitudes)

    coupling, densities = pl.pallas_call(
        functools.partial(near_kernel, s, ncpl),
        grid=(s.pairs,),
        in_specs=[smem] * 5 + [vmem] * 4 + [anywhere],
        out_specs=[square, all_dens],
        out_shape=[squares, dens_shape],
        scratch_shapes=[
            pltpu.VMEM((3 * s.pairs, s.pao, s.pao), jnp.bfloat16),
            pltpu.VMEM((ncpl * s.pao, s.pao), jnp.bfloat16),
            pltpu.VMEM((s.occ, s.pao, s.pao), jnp.float32),
            pltpu.SemaphoreType.DMA,
        ],
        compiler_params=stepped,
        cost_estimate=cost(2 * s.pairs * s.pao * s.aux * s.aux * 2, 2 * 10**7),
        name="near",
    )(
        here, pair_partner, coupling_list, lens, coupling_coef,
        pao_domain, amps_sibling, amplitudes, amps_other, dens,
    )

    some_amps, some_energies = pl.pallas_call(
        functools.partial(mid_kernel, s),
        grid=(s.pairs,),
        in_specs=[smem] * 5
        + [
            vmem,
            pl.BlockSpec((1, s.pao, s.aux), lambda p: (p, 0, 0)),
            square,
            square,
            vmem,
            anywhere,
        ],
        out_specs=[square, smem],
        out_shape=[
            jax.ShapeDtypeStruct(amplitudes.shape, amplitudes.dtype),
            jax.ShapeDtypeStruct((s.pairs,), jnp.float32),
        ],
        scratch_shapes=[
            pltpu.VMEM((s.rows + s.pao, LANES), jnp.bfloat16),
            pltpu.VMEM((s.pao, s.pao), jnp.float32),
            pltpu.SemaphoreType.DMA,
        ],
        compiler_params=stepped,
        cost_estimate=cost(2 * s.pairs * s.pao * s.pao * s.aux, 2 * 10**7),
        name="mid",
    )(
        here, pair_partner, lens, counts, offsets,
        pao_gap, aligned, coupling, amplitudes, blocks_t, from_sibling,
    )

    from_other_more = lax.cond(over, lambda a: swap(a, 1), lambda a: a, to_other_more)
    new_amps, energies = pl.pallas_call(
        functools.partial(last_kernel, s),
        in_specs=[smem] * 7 + [vmem] + [anywhere] * 6,
        out_specs=[anywhere, smem],
        out_shape=[
            jax.ShapeDtypeStruct(amplitudes.shape, amplitudes.dtype),
            jax.ShapeDtypeStruct((s.pairs,), jnp.float32),
        ],
        scratch_shapes=[
            pltpu.VMEM((s.rows + s.pao, LANES), jnp.bfloat16),
            pltpu.VMEM((s.pairs, s.pao, s.aux), jnp.bfloat16),
            pltpu.VMEM((s.pairs, s.pao, s.pao), jnp.float32),
            pltpu.VMEM((s.pairs, s.pao, s.pao), jnp.bfloat16),
            pltpu.VMEM((s.pairs, s.pao, s.pao), jnp.bfloat16),
            pltpu.VMEM((s.pao, s.pao), jnp.float32),
            pltpu.SemaphoreType.DMA((5, s.pairs)),
        ],
        input_output_aliases={13: 0},
        compiler_params=plain,
        cost_estimate=cost(2 * s.pairs * s.pao * s.pao * s.aux, 2 * 10**7),
        name="last",
    )(
        here, pair_partner, lens, counts, offsets, over.astype(jnp.int32).reshape(1), some_energies,
        pao_gap, aligned, coupling, amplitudes, from_other, from_other_more, some_amps,
    )
    return (new_amps, energies, densities)


def solution(mesh):
    return jax.shard_map(
        local,
        mesh=mesh,
        in_specs=(
            P(AXES, None, None),
            P(),
            P(),
            P(),
            P(AXES, None, None),
            P(),
            P(AXES, None),
            P(AXES, None),
        ),
        out_specs=(P(AXES, None, None), P(AXES), P(AXES, None, None)),
        check_vma=False,
    )
```

time: 116 us -> 156 us (1.34)
  blocking collectives: 0 us -> 56.1 us
  waiting for transfers between devices: 30.7 us -> 0.01 us
  Pallas kernels: 57.3 us -> 81.4 us
  starting transfers between devices: 12.2 us -> 6.41 us
  local copies, waits for them, and re-layouts: 12 us -> 9.65 us
    unnamed x0 -> x1, blocking collectives: none -> 56.1 us
    ppermute x4, waiting for transfers between devices: 30.7 us -> 0.01 us  [swap(): return lax.ppermute(array, AXES, route)]
    pallas_call x3 -> x6, Pallas kernels: 57.3 us -> 81.4 us  [the longest x1 20.8 us: local(): pl.pallas_call(functools.partial(near_kernel, s, ncpl), grid=(s.pairs,),...]
    unnamed x22 -> x34, local copies, waits for them, and re-layouts: 3.03 us -> 9.65 us
    ppermute x4, starting transfers between devices: 12.2 us -> 6.41 us  [swap(): return lax.ppermute(array, AXES, route)]
    broadcast_in_dim x6 -> x0, local copies, waits for them, and re-layouts: 4.38 us -> none  [the longest x2 2.01 us: local(): lax.dynamic_slice_in_dim(aux_domain, me * s.occ, s.occ)[:, :, None]]
    gather x4 -> x0, local copies, waits for them, and re-layouts: 2.26 us -> none  [the longest x1 0.57 us: local(): gap_left = pao_gap[own_ids][:, :, None]]
  transfers between devices with their start and end apart: 4 -> 4, of which waited for: 3 -> 0; matrix products, arithmetic and copies ran while one was open for 6% -> 2% of each run, Pallas kernels for 39% -> 47%
where the time goes in v2:
time: 156 us
  Pallas kernels  81.4 us (52%)
  blocking collectives  56.1 us (36%)
  local copies, waits for them, and re-layouts  9.65 us (6%)
  starting transfers between devices  6.41 us (4%)
  between operations  1.64 us (1%)
    unnamed x1, blocking collectives  56.1 us
    pallas_call x1, Pallas kernels, local(): pl.pallas_call(functools.partial(near_kernel, s, ncpl), grid=(s.pairs,),...  20.8 us
    pallas_call x1, Pallas kernels, local(): pl.pallas_call(functools.partial(own_kernel, s), grid=(s.pairs,), in_spec...  19.3 us
    pallas_call x1, Pallas kernels, local(): pl.pallas_call(functools.partial(pack_kernel, s), in_specs=[smem] * 3 + [...  19.1 us
    pallas_call x1, Pallas kernels, local(): pl.pallas_call(functools.partial(mid_kernel, s), grid=(s.pairs,), in_spec...  14 us
    unnamed x34, local copies, waits for them, and re-layouts  9.65 us
    pallas_call x1, Pallas kernels, local(): pl.pallas_call(functools.partial(last_kernel, s), in_specs=[smem] * 7 + [...  6.9 us
    ppermute x4, starting transfers between devices, swap(): return lax.ppermute(array, AXES, route)  6.41 us
  transfers between devices with their start and end apart: 4, of which 0 were waited for; matrix products, arithmetic and copies ran while one was open for 2% of the time, Pallas kernels for 47%

profile of v2, /device:TPU:1, one launch (start us, length us, event | category | flops | bytes accessed | tf_op | source)
XLA Modules:
  0.0 156.1 jit_solution(10812253401993881457)
XLA Ops:
  0.6 0.0 copy-start
  0.6 1.5 copy-done
  2.2 0.0 copy-start.11
  2.2 0.0 copy-start.3
  2.2 0.0 copy-start.4
  2.2 1.4 slim.1
  3.5 0.1 collective-permute-start.1
  3.6 4.4 %collective-permute-start.2 = (bf16[10,320,256]{2,1,0:T(8,128)(2,1)}, bf16[10,320,256]{2,1,0:T(8,128)(2,1)}, u32[]{:S(2)}, u32[]{:S(2)}) collective-permute-start(bf16[10,320,256]{2,1,0:T(8,128)(2,1)} %slim.1), channel_id=1, source_target_pairs={{1,2},{2,1},{3,4},{4,3},{5,6},{6,5},{7,8},{8,7},{9,10},{10,9},{11,... | collective-permute-start | bytes 4915208 | tf_op jit(solution)/shard_map/ppermute | solution.py:447
  8.1 0.0 copy-done.11
  8.1 0.1 convert_reduce_fusion.lens
  8.1 0.0 copy-done.3
  8.1 0.0 copy-done.4
  8.1 0.0 copy-start.1
  8.2 19.1 %pack.1 = (bf16[10240,128]{1,0:T(8,128)(2,1)}, bf16[5760,128]{1,0:T(8,128)(2,1)}, bf16[4480,128]{1,0:T(8,128)(2,1)}, bf16[4,1024,128]{2,1,0:T(8,128)(2,1)S(1)}, ...) custom-call(s32[1]{0:T(128)} %bitcast.here, ...), custom_call_target="tpu_custom_call" | custom-call | flops 2000000000 | bytes 10000000 | tf_op jit(solution)/shard_map/pack/pallas_call | solution.py:490
  27.3 0.0 copy-start.5
  27.3 1.0 copy-done.5
  28.2 0.0 copy-start.7
  28.2 1.0 copy-done.7
  29.2 0.0 collective-permute-start.3
  29.2 1.9 %collective-permute-start.4 = (bf16[5760,128]{1,0:T(8,128)(2,1)}, bf16[5760,128]{1,0:T(8,128)(2,1)}, u32[]{:S(2)}, u32[]{:S(2)}) collective-permute-start(bf16[5760,128]{1,0:T(8,128)(2,1)} %get-tuple-element.36), channel_id=1, source_target_pairs={{1,2},{2,1},{3,4},{4,3},{5,6},{6,5},{7,8},{8,7},{9,10},{10,9},{11,... | collective-permute-start | bytes 4423688 | tf_op jit(solution)/shard_map/ppermute | solution.py:447
  31.1 0.2 slice_dynamic-update-slice_fusion
  31.3 0.0 copy-done.1
  31.3 0.0 copy-start.6
  31.3 1.2 copy-done.6
  32.5 0.0 copy-start.8
  32.6 1.2 copy-done.8
  33.8 0.0 copy-start.12
  33.8 19.3 %own.2 = (bf16[8,320,1024]{2,1,0:T(8,128)(2,1)}, f32[4,320,320]{2,1,0:T(8,128)S(1)}) custom-call(s32[1]{0:T(128)} %bitcast.here, s32[256]{0:T(256)S(1)} %copy-done.3, s32[128]{0:T(128)S(1)} %convert_reduce_fusion.lens, s32[12]{0:T(128)S(1)} %get-tuple-element.25.counts, bf16[12,32,128]{2,1,0:T(8,128)(2,1)S(1)} %get-tuple-element.28.tables, ...), custom_call_target="tpu_custom_call" | custom-call | flops 10737418240 | bytes 20000000 | tf_op jit(solution)/shard_map/own/pallas_call | solution.py:524
  53.1 1.3 copy-done.9
  54.4 56.1 %all-reduce = s32[32]{0:T(128)S(1)} all-reduce(s32[32]{0:T(128)S(1)} %slice_dynamic-update-slice_fusion), channel_id=1, replica_groups=mesh['orb'=4,'pair'=8] {'orb','pair'}, use_global_device_ids=true, to_apply=%add | all-reduce | flops 32 | bytes 256
  110.4 1.0 copy.14.pao_rows
  111.5 0.0 copy-done.12
  111.5 0.1 copy.12.listed
  111.6 0.0 copy-done.13
  111.6 0.1 copy.13.coef
  111.7 1.0 copy.15.gaps
  112.7 0.6 reduce_max.9
  114.0 0.0 copy-done.10
  114.0 0.2 conditional.1
  114.2 0.0 collective-permute-done.1.sibling
  114.2 0.0 collective-permute-done.2.other
  114.2 0.0 copy-start.2
  114.2 20.8 %near.1 = (f32[8,320,320]{2,1,0:T(8,128)}, f32[4,320,320]{2,1,0:T(8,128)}) custom-call(s32[1]{0:T(128)} %bitcast.here, s32[256]{0:T(256)S(1)} %copy-done.3, s32[8,4]{1,0:T(8,128)S(1)} %copy.12.listed, s32[128]{0:T(128)S(1)} %convert_reduce_fusion.lens, f32[8,4]{1,0:T(8,128)S(1)} %copy.13.coef, s32[128,320]{1,0:T(8,128)S(1)} %copy.14.pao_rows, ...), custom_call_target="tpu_custom_call" | custom-call | flops 10737418240 | bytes 20000000 | tf_op jit(solution)/shard_map/near/pallas_call | solution.py:548
  135.0 0.0 collective-permute-done.3.sibling
  135.0 0.0 copy-done.2
  135.0 14.0 %mid.1 = (bf16[8,320,320]{2,1,0:T(8,128)(2,1)}, f32[8]{0:T(128)S(1)}) custom-call(s32[1]{0:T(128)} %bitcast.here, s32[256]{0:T(256)S(1)} %copy-done.3, s32[128]{0:T(128)S(1)} %convert_reduce_fusion.lens, s32[12]{0:T(128)S(1)} %get-tuple-element.25.counts, s32[12]{0:T(128)S(1)} %get-tuple-element.26.offsets, f32[128,320]{1,0:T(8,128)S(1)} %copy.15.gaps, ...), custom_call_target="tpu_custom_call" | custom-call | flops 1677721600 | bytes 20000000 | tf_op jit(solution)/shard_map/mid/pallas_call | solution.py:568
  149.0 0.0 collective-permute-done.4.other
  149.0 6.9 %last.1 = (bf16[8,320,320]{2,1,0:T(8,128)(2,1)}, f32[8]{0:T(128)}) custom-call(s32[1]{0:T(128)} %bitcast.here, s32[256]{0:T(256)S(1)} %copy-done.3, s32[128]{0:T(128)S(1)} %convert_reduce_fusion.lens, s32[12]{0:T(128)S(1)} %get-tuple-element.25.counts, s32[12]{0:T(128)S(1)} %get-tuple-element.26.offsets, ...), custom_call_target="tpu_custom_call", output_to_operand_aliasing={{0}: (13, {})} | custom-call | flops 1677721600 | bytes 20000000 | tf_op jit(solution)/shard_map/last/pallas_call | solution.py:599
  (4 shorter events, 0.0 us)
Async XLA Ops:
  0.6 1.5 copy-start
  2.2 5.9 %copy-start.11 = (s32[128,320]{0,1:T(8,128)S(1)}, s32[128,320]{0,1:T(8,128)}, u32[]{:S(2)}) copy-start(s32[128,320]{0,1:T(8,128)} %param.12) | copy-start | bytes 491524
  2.2 5.9 %copy-start.3 = (s32[256]{0:T(256)S(1)}, s32[256]{0:T(256)}, u32[]{:S(2)}) copy-start(s32[256]{0:T(256)} %partner.9) | copy-start | bytes 3076
  2.2 6.0 %copy-start.4 = (s32[128,1024]{1,0:T(8,128)S(1)}, s32[128,1024]{1,0:T(8,128)}, u32[]{:S(2)}) copy-start(s32[128,1024]{1,0:T(8,128)} %aux_rows.1) | copy-start | bytes 1572868
  3.5 110.7 %collective-permute-start.1 = (bf16[10,320,256]{2,1,0:T(8,128)(2,1)}, bf16[10,320,256]{2,1,0:T(8,128)(2,1)}, u32[]{:S(2)}, u32[]{:S(2)}) collective-permute-start(bf16[10,320,256]{2,1,0:T(8,128)(2,1)} %slim.1), channel_id=1, source_target_pairs={{0,1},{1,0},{2,3},{3,2},{4,5},{5,4},{6,7},{7,6},{8,9},{9,8},{10,11... | collective-permute-start | bytes 4915208 | tf_op jit(solution)/shard_map/ppermute | solution.py:447
  3.6 110.6 %collective-permute-start.2 = (bf16[10,320,256]{2,1,0:T(8,128)(2,1)}, bf16[10,320,256]{2,1,0:T(8,128)(2,1)}, u32[]{:S(2)}, u32[]{:S(2)}) collective-permute-start(bf16[10,320,256]{2,1,0:T(8,128)(2,1)} %slim.1), channel_id=1, source_target_pairs={{1,2},{2,1},{3,4},{4,3},{5,6},{6,5},{7,8},{8,7},{9,10},{10,9},{11,... | collective-permute-start | bytes 4915208 | tf_op jit(solution)/shard_map/ppermute | solution.py:447
  8.1 23.2 %copy-start.1 = (bf16[8,320,320]{2,1,0:T(8,128)(2,1)S(1)}, bf16[8,320,320]{2,1,0:T(8,128)(2,1)}, u32[]{:S(2)}) copy-start(bf16[8,320,320]{2,1,0:T(8,128)(2,1)} %amps.7) | copy-start | bytes 4915204
  27.3 1.0 copy-start.5
  28.2 1.0 copy-start.7
  29.2 105.8 %collective-permute-start.3 = (bf16[10240,128]{1,0:T(8,128)(2,1)}, bf16[10240,128]{1,0:T(8,128)(2,1)}, u32[]{:S(2)}, u32[]{:S(2)}) collective-permute-start(bf16[10240,128]{1,0:T(8,128)(2,1)} %get-tuple-element.34), channel_id=1, source_target_pairs={{0,1},{1,0},{2,3},{3,2},{4,5},{5,4},{6,7},{7,6},{8,9},{9,8},{10,11... | collective-permute-start | bytes 7864328 | tf_op jit(solution)/shard_map/ppermute | solution.py:447
  29.2 119.8 %collective-permute-start.4 = (bf16[5760,128]{1,0:T(8,128)(2,1)}, bf16[5760,128]{1,0:T(8,128)(2,1)}, u32[]{:S(2)}, u32[]{:S(2)}) collective-permute-start(bf16[5760,128]{1,0:T(8,128)(2,1)} %get-tuple-element.36), channel_id=1, source_target_pairs={{1,2},{2,1},{3,4},{4,3},{5,6},{6,5},{7,8},{8,7},{9,10},{10,9},{11,... | collective-permute-start | bytes 4423688 | tf_op jit(solution)/shard_map/ppermute | solution.py:447
  31.3 1.2 copy-start.6
  32.5 1.2 copy-start.8
  33.8 77.7 %copy-start.12 = (s32[8,4]{0,1:T(4,128)S(1)}, s32[8,4]{0,1:T(4,128)}, u32[]{:S(2)}) copy-start(s32[8,4]{0,1:T(4,128)} %param.16) | copy-start | bytes 388
  33.8 77.8 %copy-start.13 = (f32[8,4]{0,1:T(4,128)S(1)}, f32[8,4]{0,1:T(4,128)}, u32[]{:S(2)}) copy-start(f32[8,4]{0,1:T(4,128)} %param.17) | copy-start | bytes 388
  33.8 80.2 %copy-start.10 = (bf16[4480,128]{1,0:T(8,128)(2,1)S(1)}, bf16[4480,128]{1,0:T(8,128)(2,1)}, u32[]{:S(2)}) copy-start(bf16[4480,128]{1,0:T(8,128)(2,1)} %get-tuple-element.37) | copy-start | bytes 3440644
  53.1 1.3 copy-start.9
  114.2 20.8 %copy-start.2 = (bf16[4,1024,320]{1,2,0:T(8,128)(2,1)S(1)}, bf16[4,1024,320]{1,2,0:T(8,128)(2,1)}, u32[]{:S(2)}) copy-start(bf16[4,1024,320]{1,2,0:T(8,128)(2,1)} %param.10) | copy-start | bytes 7864324

commit v3 on v2

--- a/solution.py
+++ b/solution.py
@@ -8,7 +8,7 @@
 from jax.sharding import PartitionSpec as P
 
 AXES = ("orb", "pair")
-VMEM_BYTES = 48 * 1024 * 1024
+VMEM_BYTES = 60 * 1024 * 1024
 AUX_IDS = 2048
 LOW = 64
 HIGH = AUX_IDS // LOW
@@ -40,6 +40,11 @@
     return jnp.where(live(rows, cols, amp.shape), amp.astype(jnp.float32), 0.0).astype(amp.dtype)
 
 
+def short_where(equal):
+    one = jnp.ones(equal.shape, jnp.bfloat16)
+    return jnp.where(equal, one, jnp.zeros_like(one))
+
+
 def column(row):
     return jnp.broadcast_to(row, (LANES, row.shape[1])).T
 
@@ -48,7 +53,8 @@
     parts = []
     for at in range(0, row.shape[1], LANES):
         piece = row[:, at : at + LANES]
-        parts.append(one_where(col[:, : piece.shape[1]] == piece))
+        wide = jnp.broadcast_to(piece, (col.shape[0], piece.shape[1]))
+        parts.append(short_where(col[:, : piece.shape[1]] == wide))
     return jnp.concatenate(parts, axis=1)
 
 
@@ -109,69 +115,123 @@
     out[:, whole:] = packed[s.pairs + k // share, :, spot : spot + tail]
 
 
-def places(high, weight, table):
-    found = dot(high[:, :HIGH], table).astype(jnp.bfloat16) * weight
-    return dot(found, jnp.ones((LANES, LANES), jnp.bfloat16))
+def bits(values, count, lanes):
+    levels = iota((count, lanes), 0).astype(jnp.bfloat16)
+    return short_where(levels == jnp.broadcast_to(values.astype(jnp.bfloat16), (count, lanes)))
+
+
+def places(row, table):
+    found = dot(table, bits(row // LOW, HIGH, row.shape[1]))
+    low = bits(lax.rem(row, LOW), LOW, row.shape[1]).astype(jnp.float32)
+    return jnp.sum((found[:LOW] * BASE + found[LOW:]) * low, axis=0, keepdims=True)
 
 
 def picker(place, chunk):
-    spot = iota(place.shape, 1).astype(jnp.float32) + (chunk * LANES + 1).astype(jnp.float32)
-    return jnp.concatenate([one_where(place == spot), one_where(place == spot + LANES)], axis=1)
-
-
-def split_place(place, lane):
-    part = jnp.where(lane < LOW, place // BASE, lax.rem(place, BASE))
-    return part.astype(jnp.float32)
+    wide = 2 * LANES
+    middle = chunk * wide + LANES + 1
+    spot = (place - jnp.asarray(middle).astype(jnp.float32)).astype(jnp.bfloat16)
+    levels = (iota((wide, place.shape[1]), 0) - LANES).astype(jnp.bfloat16)
+    return short_where(levels == jnp.broadcast_to(spot, levels.shape))
+
+
+def chunkwise(s, count, act):
+    for c in range(s.aux // (2 * LANES)):
+        pl.when(count > c * 2 * LANES)(functools.partial(act, c))
+
+
+def split_place(place, row):
+    part = jnp.where(row < LOW, place // BASE, lax.rem(place, BASE))
+    return part.astype(jnp.float32).astype(jnp.bfloat16)
 
 
 def pack_kernel(
-    s, here, partner, lens, aux_rows, blocks, to_sibling, to_other, to_other_more, high, weight, tables, counts, offsets, load, maps, sends, bufs, sems
+    s, here, partner, lens, aux_rows, blocks, pao_cols, gap_cols, to_sibling, to_other, to_other_more, tables, pao_rows, gap_rows, counts, offsets, maps, sends, bufs, sems
 ):
     me = here[0]
     peers = swapped(me)
+    pao_rows[...] = pao_cols[...].T
+    gap_rows[...] = gap_cols[...].T
 
     for g, device in enumerate((me,) + peers):
         for k in range(s.occ):
             orbital = jnp.clip(device * s.occ + k, 0, s.nocc - 1)
             row = aux_rows[pl.ds(orbital, 1), :]
-            lane = iota((LANES, s.aux), 0)
-            matches = lax.rem(lane, LOW) == lax.rem(row, LOW)
-            by_high = one_where(iota((HIGH, s.aux), 0) == row // LOW)
-            maps[g * s.occ + k] = dot(by_high, one_where(matches), NT)
+            by_high = bits(row // LOW, HIGH, s.aux)
+            by_low = bits(lax.rem(row, LOW), LOW, s.aux)
+            maps[g * s.occ + k] = dot(jnp.concatenate([by_low, by_low], axis=0), by_high, NT)
             if g == 0:
-                spot = split_place(iota((LANES, s.aux), 1) + 1, lane)
-                table = dot(by_high, one_where(matches, spot), NT)
-                tables[2 * s.occ + k] = table.astype(jnp.bfloat16)
-                col = column(row)
-                lane = iota((s.aux, LANES), 1)
-                high[k] = one_where(col // LOW == lane)
-                weight[k] = one_where(
-                    lax.rem(col, LOW) == lax.rem(lane, LOW), jnp.where(lane < LOW, 1.0 * BASE, 1.0)
+                spot = iota((LOW, s.aux), 1) + 1
+                parts = jnp.concatenate(
+                    [
+                        (spot // BASE).astype(jnp.float32).astype(jnp.bfloat16) * by_low,
+                        lax.rem(spot, BASE).astype(jnp.float32).astype(jnp.bfloat16) * by_low,
+                    ],
+                    axis=0,
                 )
-
-    lane_in, lane_out = iota((LANES, LANES), 0), iota((LANES, LANES), 1)
-    ahead = one_where((lane_in < LOW) & (lane_in < lax.rem(lane_out, LOW)))
-    first = one_where(lane_in < LOW)
-    above = one_where(iota((HIGH, HIGH), 1) < iota((HIGH, HIGH), 0))
-    lane = iota((HIGH, LANES), 1)
+                tables[2 * s.occ + k] = dot(parts, by_high, NT).astype(jnp.bfloat16)
+
+    sub, lane = iota((2 * LOW, 2 * LOW), 0), iota((2 * LOW, 2 * LOW), 1)
+    ahead = one_where((lane < LOW) & (lane < lax.rem(sub, LOW)))
+    first = one_where(lane < LOW)
+    above = one_where(iota((HIGH, HIGH), 0) < iota((HIGH, HIGH), 1))
+    level = iota((2 * LOW, HIGH), 0)
 
     def listing(target, users, device, orbital):
-        union = jnp.zeros((HIGH, LANES), jnp.float32)
-        for q in range(s.pairs):
-            pair = device * s.pairs + q
-            inside = (pair >= 0) & (pair < s.npair)
-            uses = inside & (partner[jnp.clip(pair, 0, s.npair - 1)] == orbital)
-            union += jnp.where(uses, 1.0, 0.0) * maps[users + q % s.occ]
+        union = jnp.zeros((2 * LOW, HIGH), jnp.float32)
+        for q in range(s.occ):
+            uses = jnp.bool_(False)
+            for pair in range(q, s.pairs, s.occ):
+                pair += device * s.pairs
+                inside = (pair >= 0) & (pair < s.npair)
+                uses |= inside & (partner[jnp.clip(pair, 0, s.npair - 1)] == orbital)
+            union += jnp.where(uses, 1.0, 0.0) * maps[users + q]
         taken = (union > 0.0) & (maps[target] > 0.0)
         flags = one_where(taken)
-        total = dot(flags, first)
-        place = dot(flags, ahead) + dot(above, total.astype(jnp.bfloat16)) + 1.0
+        total = dot(first, flags)
+        place = dot(ahead, flags) + dot(total.astype(jnp.bfloat16), above) + 1.0
         place = jnp.where(taken, place, 0.0).astype(jnp.int32)
-        count = jnp.sum(jnp.where(lane == 0, total, 0.0)).astype(jnp.int32)
-        return split_place(place, lane).astype(jnp.bfloat16), count
+        count = jnp.sum(total[:1]).astype(jnp.int32)
+        return split_place(place, level), count
+
+    copies = {
+        0: [pltpu.make_async_copy(bufs.at[0, pl.ds(0, s.rows)], to_sibling, sems.at[0])],
+        1: [
+            pltpu.make_async_copy(bufs.at[1, pl.ds(0, s.first)], to_other, sems.at[1]),
+            pltpu.make_async_copy(
+                bufs.at[1, pl.ds(s.first, s.rows - s.first)], to_other_more, sems.at[2]
+            ),
+        ],
+    }
+    for r in (1, 0):
+        listed = []
+        at = jnp.int32(0)
+        for k in range(s.occ):
+            sends[k], count = listing(k, (1 + r) * s.occ, peers[r], me * s.occ + k)
+            step = rows_of(lens[me * s.occ + k])
+            listed.append((at, step, count))
+            at += chunks_of(count) * step
+        for k, (at, step, count) in enumerate(listed):
+
+            @pl.when(count > 0)
+            def _(k=k, at=at, step=step, count=count):
+                place = places(aux_rows[pl.ds(me * s.occ + k, 1), :], sends[k])
+
+                def some(c):
+                    got = dot(blocks[k], picker(place, c), NT).astype(jnp.bfloat16)
+                    spot = pl.multiple_of(at + 2 * c * step, 16)
+                    bufs[r, pl.ds(spot, s.pao), :] = got[:, :LANES]
+
+                    @pl.when((2 * c + 1) * LANES < count)
+                    def _():
+                        bufs[r, pl.ds(pl.multiple_of(spot + step, 16), s.pao), :] = got[:, LANES:]
+
+                chunkwise(s, count, some)
+
+        for copy in copies[r]:
+            copy.start()
 
     for r in range(2):
-        at, load[r] = jnp.int32(0), jnp.int32(0)
+        at = jnp.int32(0)
         for k in range(s.occ):
             l = r * s.occ + k
             orbital = jnp.clip(peers[r] * s.occ + k, 0, s.nocc - 1)
@@ -182,65 +242,74 @@
         counts[2 * s.occ + k] = jnp.int32(s.aux)
         offsets[2 * s.occ + k] = jnp.int32(0)
 
-    copies = []
-    for r in (1, 0):
-        at = jnp.int32(0)
+    for copy in copies[1] + copies[0]:
+        copy.wait()
+
+
+def count_kernel(s, partner, lens, aux_rows, over, maps, sums, steps):
+    high = AUX_IDS // LANES
+    group = 8
+
+    def some(g, _):
+        rows = aux_rows[pl.ds(pl.multiple_of(g * group, group), group), :]
+        for t in range(group):
+            row = rows[t : t + 1]
+            by_low = bits(lax.rem(row, LANES), LANES, s.aux)
+            maps[g * group + t] = dot(bits(row // LANES, high, s.aux), by_low, NT)
+        return 0
+
+    lax.fori_loop(0, s.nocc // group, some, 0)
+
+    sums[...] = jnp.zeros_like(sums)
+    steps[...] = jnp.zeros_like(steps)
+    devices = s.nocc // s.occ
+
+    def edge(e, _):
+        source = e + 1
+        user = source + 1 - 2 * lax.rem(e, 2)
         for k in range(s.occ):
-            table, count = listing(k, (1 + r) * s.occ, peers[r], me * s.occ + k)
-            sends[k] = table
-            step = rows_of(lens[me * s.occ + k])
-
-            @pl.when(count > 0)
-            def _(k=k, at=at, step=step, count=count):
-                place = places(high[k], weight[k], sends[k])
-
-                def some(c, _):
-                    got = dot(blocks[k], picker(place, 2 * c)).astype(jnp.bfloat16)
-                    spot = pl.multiple_of(at + 2 * c * step, 16)
-                    bufs[r, pl.ds(spot, s.pao), :] = got[:, :LANES]
-
-                    @pl.when((2 * c + 1) * LANES < count)
-                    def _():
-                        bufs[r, pl.ds(pl.multiple_of(spot + step, 16), s.pao), :] = got[:, LANES:]
-
-                    return 0
-
-                lax.fori_loop(0, (chunks_of(count) + 1) // 2, some, 0)
-
-            at += chunks_of(count) * step
-        load[r] = at
-        if r == 1:
-            copies = [
-                pltpu.make_async_copy(bufs.at[1, pl.ds(0, s.first)], to_other, sems.at[0]),
-                pltpu.make_async_copy(
-                    bufs.at[1, pl.ds(s.first, s.rows - s.first)], to_other_more, sems.at[1]
-                ),
-            ]
-        else:
-            copies = [pltpu.make_async_copy(bufs.at[0, pl.ds(0, s.rows)], to_sibling, sems.at[2])]
-        for copy in copies:
-            copy.start()
-        if r == 1:
-            pending = copies
-    for copy in pending + copies:
-        copy.wait()
-
-
-def own_kernel(s, here, partner, lens, counts, tables, blocks, high, weight, amps, aligned, dens):
+            orbital = source * s.occ + k
+            union = jnp.zeros((high, LANES), jnp.float32)
+            for q in range(s.occ):
+                uses = jnp.bool_(False)
+                for pair in range(q, s.pairs, s.occ):
+                    uses |= partner[user * s.pairs + pair] == orbital
+                union += jnp.where(uses, 1.0, 0.0) * maps[user * s.occ + q]
+            taken = jnp.where((union > 0.0) & (maps[orbital] > 0.0), 1.0, 0.0)
+            sums[k, pl.ds(e, 1), :] = jnp.sum(taken, axis=0, keepdims=True)
+            steps[k, pl.ds(e, 1), :] = jnp.full(
+                (1, LANES), rows_of(lens[orbital]).astype(jnp.float32), jnp.float32
+            )
+        return 0
+
+    lax.fori_loop(0, devices - 2, edge, 0)
+    need = jnp.zeros(sums.shape[1:], jnp.float32)
+    ones = jnp.ones((LANES, LANES), jnp.bfloat16)
+    for k in range(s.occ):
+        count = dot(sums[k].astype(jnp.bfloat16), ones)
+        need += jnp.floor((count + (LANES - 1)) / LANES) * steps[k]
+    over[0] = (jnp.max(need) > s.first).astype(jnp.int32)
+
+
+def own_kernel(s, here, partner, lens, counts, tables, aux_rows, blocks, amps, aligned, dens):
     g = pl.program_id(0)
     me = here[0]
     left, p = paired(s, g)
     right = partner[me * s.pairs + p]
+    l, _ = s.where_partner(me, right)
+    count = counts[l]
+    place = places(aux_rows[pl.ds(me * s.occ + left, 1), :], tables[l])
     wide = 2 * LANES
-    l, _ = s.where_partner(me, right)
-    place = places(high[0], weight[0], tables[l])
-
-    def some(c, _):
-        at = pl.multiple_of(c * wide, wide)
-        aligned[0, :, pl.ds(at, wide)] = dot(blocks[0], picker(place, 2 * c)).astype(jnp.bfloat16)
-        return 0
-
-    lax.fori_loop(0, (chunks_of(counts[l]) + 1) // 2, some, 0)
+
+    def some(c):
+        aligned[0, :, c * wide : (c + 1) * wide] = dot(
+            blocks[0], picker(place, c), NT
+        ).astype(jnp.bfloat16)
+
+    chunks = s.aux // wide
+    for c in range(chunks - 1):
+        some(c)
+    pl.when(count > (chunks - 1) * wide)(functools.partial(some, chunks - 1))
 
     masked = kept(amps[0], lens[me * s.occ + left], lens[right])
     term = dot(masked, masked, NT)
@@ -282,7 +351,7 @@
 
     def column_of(orbital):
         row = row_of(orbital)
-        return column(jnp.where(row < 0, -2, row))
+        return column(jnp.where(row < 0, -2, row)).astype(jnp.int16)
 
     right_col = column_of(partner[me * s.pairs + p])
     left_col = column_of(me * s.occ + lax.rem(p, s.occ))
@@ -291,9 +360,10 @@
         m = listed[p, c]
         left_rows.append(row_of(s.first_orbital(m)))
         amp = wide[m - (me - 1) * s.pairs]
-        moved = dot(amp, same(right_col, row_of(partner[m])), NT)
+        moved = dot(amp, same(right_col, row_of(partner[m]).astype(jnp.int16)), NT)
         tall[c * s.pao : (c + 1) * s.pao] = (coef[p, c] * moved).astype(jnp.bfloat16)
-    coupling[0] = dot(same(left_col, jnp.concatenate(left_rows, axis=1)), tall[...])
+    left_row = jnp.concatenate(left_rows, axis=1).astype(jnp.int16)
+    coupling[0] = dot(same(left_col, left_row), tall[...])
 
     for side in range(3):
         m = (me + side - 1) * s.pairs + p
@@ -329,19 +399,25 @@
 
 
 def compacted(s, count, at, step, aligned, halo, sums):
-    sums[...] = jnp.zeros_like(sums)
     wide = 2 * LANES
 
-    def some(c, _):
+    def some(c):
         spot = pl.multiple_of(at + 2 * c * step, 16)
         one = halo[pl.ds(spot, s.pao), :]
         two = halo[pl.ds(pl.multiple_of(spot + step, 16), s.pao), :]
         two = jnp.where((2 * c + 1) * LANES < count, two, jnp.zeros_like(two))
-        lanes = pl.ds(pl.multiple_of(c * wide, wide), wide)
-        sums[...] += dot(aligned[:, lanes], jnp.concatenate([one, two], axis=1), NT)
-        return 0
-
-    lax.fori_loop(0, (chunks_of(count) + 1) // 2, some, 0)
+        both = jnp.concatenate([one, two], axis=1)
+        term = dot(aligned[:, c * wide : (c + 1) * wide], both, NT)
+        if c == 0:
+            sums[...] = term
+        else:
+            sums[...] += term
+
+    @pl.when(count == 0)
+    def _():
+        sums[...] = jnp.zeros_like(sums)
+
+    chunkwise(s, count, some)
 
 
 def mid_kernel(
@@ -437,6 +513,10 @@
     each(lambda p, right, l: result(p).wait())
 
 
+def position():
+    return lax.axis_index(AXES)
+
+
 def swap(array, role):
     count = 1
     for axis in AXES:
@@ -452,7 +532,7 @@
 ):
     s = Sizes(blocks, amplitudes, pair_partner)
     ncpl = coupling_list.shape[1]
-    me = lax.axis_index(AXES)
+    me = position()
     here = me.astype(jnp.int32).reshape(1)
     blocks_t = jnp.swapaxes(blocks, 1, 2)
 
@@ -486,39 +566,52 @@
 
     lens = jnp.sum((pao_domain >= 0).astype(jnp.int32), axis=1)
 
-    tables_number = 3 * s.occ
-    to_sibling, to_other, to_other_more, high, weight, tables, counts, offsets, load = pl.pallas_call(
+    lists = 3 * s.occ
+    to_sibling, to_other, to_other_more, tables, pao_rows, gap_rows, counts, offsets = pl.pallas_call(
         functools.partial(pack_kernel, s),
-        in_specs=[smem] * 3 + [vmem] * 2,
-        out_specs=[anywhere] * 3 + [vmem] * 3 + [smem] * 3,
+        in_specs=[smem] * 3 + [vmem] * 4,
+        out_specs=[anywhere] * 3 + [vmem] * 3 + [smem] * 2,
         out_shape=[
             jax.ShapeDtypeStruct((s.rows, LANES), jnp.bfloat16),
             jax.ShapeDtypeStruct((s.first, LANES), jnp.bfloat16),
             jax.ShapeDtypeStruct((s.rows - s.first, LANES), jnp.bfloat16),
-            jax.ShapeDtypeStruct((s.occ, s.aux, LANES), jnp.bfloat16),
-            jax.ShapeDtypeStruct((s.occ, s.aux, LANES), jnp.bfloat16),
-            jax.ShapeDtypeStruct((tables_number, HIGH, LANES), jnp.bfloat16),
-            jax.ShapeDtypeStruct((tables_number,), jnp.int32),
-            jax.ShapeDtypeStruct((tables_number,), jnp.int32),
-            jax.ShapeDtypeStruct((2,), jnp.int32),
+            jax.ShapeDtypeStruct((lists, 2 * LOW, HIGH), jnp.bfloat16),
+            jax.ShapeDtypeStruct(pao_domain.shape, pao_domain.dtype),
+            jax.ShapeDtypeStruct(pao_gap.shape, pao_gap.dtype),
+            jax.ShapeDtypeStruct((lists,), jnp.int32),
+            jax.ShapeDtypeStruct((lists,), jnp.int32),
         ],
         scratch_shapes=[
-            pltpu.VMEM((3 * s.occ, HIGH, LANES), jnp.float32),
-            pltpu.VMEM((s.occ, HIGH, LANES), jnp.bfloat16),
+            pltpu.VMEM((3 * s.occ, 2 * LOW, HIGH), jnp.float32),
+            pltpu.VMEM((s.occ, 2 * LOW, HIGH), jnp.bfloat16),
             pltpu.VMEM((2, s.rows + s.pao, LANES), jnp.bfloat16),
             pltpu.SemaphoreType.DMA((3,)),
         ],
         compiler_params=plain,
         cost_estimate=cost(2 * 10**9, 10**7),
         name="pack",
-    )(here, pair_partner, lens, aux_domain, blocks_t)
+    )(here, pair_partner, lens, aux_domain, blocks_t, pao_domain.T, pao_gap.T)
 
     from_other = swap(to_other, 1)
     from_sibling = swap(to_sibling, 0)
-    loads = lax.all_gather(load[1:], AXES, tiled=True)
-    over = jnp.max(loads) > s.first
-
-    def by_left(block, *rest):
+
+    edges = -(-(s.nocc // s.occ) // 8) * 8
+    (over,) = pl.pallas_call(
+        functools.partial(count_kernel, s),
+        in_specs=[smem] * 2 + [vmem],
+        out_specs=[smem],
+        out_shape=[jax.ShapeDtypeStruct((1,), jnp.int32)],
+        scratch_shapes=[
+            pltpu.VMEM((s.nocc, AUX_IDS // LANES, LANES), jnp.float32),
+            pltpu.VMEM((s.occ, edges, LANES), jnp.float32),
+            pltpu.VMEM((s.occ, edges, LANES), jnp.float32),
+        ],
+        compiler_params=plain,
+        cost_estimate=cost(10**9, 10**6),
+        name="count",
+    )(pair_partner, lens, aux_domain)
+
+    def by_left(block):
         return pl.BlockSpec((1,) + block, lambda g: (paired(s, g)[0], 0, 0))
 
     aligned, dens = pl.pallas_call(
@@ -527,9 +620,8 @@
         in_specs=[smem] * 4
         + [
             vmem,
+            vmem,
             by_left((s.pao, s.aux)),
-            by_left((s.aux, LANES)),
-            by_left((s.aux, LANES)),
             pl.BlockSpec((1, s.pao, s.pao), lambda g: (paired(s, g)[1], 0, 0)),
         ],
         out_specs=[
@@ -543,7 +635,7 @@
         compiler_params=stepped,
         cost_estimate=cost(2 * s.pairs * s.pao * s.aux * s.aux * 2, 2 * 10**7),
         name="own",
-    )(here, pair_partner, lens, counts, tables, blocks_t, high, weight, amplitudes)
+    )(here, pair_partner, lens, counts, tables, aux_domain, blocks_t, amplitudes)
 
     coupling, densities = pl.pallas_call(
         functools.partial(near_kernel, s, ncpl),
@@ -562,7 +654,7 @@
         name="near",
     )(
         here, pair_partner, coupling_list, lens, coupling_coef,
-        pao_domain, amps_sibling, amplitudes, amps_other, dens,
+        pao_rows, amps_sibling, amplitudes, amps_other, dens,
     )
 
     some_amps, some_energies = pl.pallas_call(
@@ -592,10 +684,10 @@
         name="mid",
     )(
         here, pair_partner, lens, counts, offsets,
-        pao_gap, aligned, coupling, amplitudes, blocks_t, from_sibling,
+        gap_rows, aligned, coupling, amplitudes, blocks_t, from_sibling,
     )
 
-    from_other_more = lax.cond(over, lambda a: swap(a, 1), lambda a: a, to_other_more)
+    from_other_more = lax.cond(over[0] > 0, lambda a: swap(a, 1), lambda a: a, to_other_more)
     new_amps, energies = pl.pallas_call(
         functools.partial(last_kernel, s),
         in_specs=[smem] * 7 + [vmem] + [anywhere] * 6,
@@ -618,8 +710,8 @@
         cost_estimate=cost(2 * s.pairs * s.pao * s.pao * s.aux, 2 * 10**7),
         name="last",
     )(
-        here, pair_partner, lens, counts, offsets, over.astype(jnp.int32).reshape(1), some_energies,
-        pao_gap, aligned, coupling, amplitudes, from_other, from_other_more, some_amps,
+        here, pair_partner, lens, counts, offsets, over, some_energies,
+        gap_rows, aligned, coupling, amplitudes, from_other, from_other_more, some_amps,
     )
     return (new_amps, energies, densities)
 

time: 156 us -> 105 us (0.67)
  the two profiles are of different devices: /device:TPU:1 before, /device:TPU:21 now
where the time goes in v3:
time: 105 us; the launch traced here: 103 us
  Pallas kernels  86.1 us (82%)
  starting transfers between devices  8.59 us (8%)
  waiting for transfers between devices  3.48 us (3%)
  local copies, waits for them, and re-layouts  2.83 us (3%)
  between operations  1.55 us (1%)
    pallas_call x1, Pallas kernels, local(): pl.pallas_call(functools.partial(near_kernel, s, ncpl), grid=(s.pairs,),...  20.7 us
    pallas_call x1, Pallas kernels, local(): pl.pallas_call(functools.partial(own_kernel, s), grid=(s.pairs,), in_spec...  14.8 us
    pallas_call x1, Pallas kernels, local(): pl.pallas_call(functools.partial(count_kernel, s), in_specs=[smem] * 2 +...  14.6 us
    pallas_call x1, Pallas kernels, local(): pl.pallas_call(functools.partial(mid_kernel, s), grid=(s.pairs,), in_spec...  13.3 us
    pallas_call x1, Pallas kernels, local(): pl.pallas_call(functools.partial(pack_kernel, s), in_specs=[smem] * 3 + [...  13 us
    ppermute x4, starting transfers between devices, swap(): return lax.ppermute(array, AXES, route)  8.59 us
    pallas_call x1, Pallas kernels, local(): pl.pallas_call(functools.partial(last_kernel, s), in_specs=[smem] * 7 + [...  6.76 us
    ppermute x4, waiting for transfers between devices, swap(): return lax.ppermute(array, AXES, route)  3.48 us
  transfers between devices with their start and end apart: 4, of which 1 were waited for; matrix products, arithmetic and copies ran while one was open for 2% of the time, Pallas kernels for 74%

profile of v3, /device:TPU:21, one launch (start us, length us, event | category | flops | bytes accessed | tf_op | source)
XLA Modules:
  0.0 103.1 jit_solution(6830983129662341597)
XLA Ops:
  0.6 0.0 copy-start.2
  0.6 2.9 %slim.1 = bf16[10,320,256]{2,1,0:T(8,128)(2,1)} custom-call(bf16[8,320,320]{2,1,0:T(8,128)(2,1)} %amps.7), custom_call_target="tpu_custom_call" | custom-call | flops 1000000 | bytes 4000000 | tf_op jit(solution)/shard_map/slim/pallas_call | solution.py:555
  3.6 0.7 collective-permute-start.1
  4.2 3.0 %collective-permute-start.2 = (bf16[10,320,256]{2,1,0:T(8,128)(2,1)}, bf16[10,320,256]{2,1,0:T(8,128)(2,1)}, u32[]{:S(2)}, u32[]{:S(2)}) collective-permute-start(bf16[10,320,256]{2,1,0:T(8,128)(2,1)} %slim.1), channel_id=1, source_target_pairs={{1,2},{2,1},{3,4},{4,3},{5,6},{6,5},{7,8},{8,7},{9,10},{10,9},{11,... | collective-permute-start | bytes 4915208 | tf_op jit(solution)/shard_map/ppermute | solution.py:527
  7.3 0.0 copy-done.2
  7.3 0.6 convert_reduce_fusion.lens
  7.8 13.0 %pack.1 = (bf16[10240,128]{1,0:T(8,128)(2,1)}, bf16[5760,128]{1,0:T(8,128)(2,1)}, bf16[4480,128]{1,0:T(8,128)(2,1)}, bf16[12,128,32]{2,1,0:T(8,128)(2,1)}, s32[1...) custom-call(s32[1]{0:T(128)} %bitcast.here, s32[256]{0:T(256)} %partner.11, ...), custom_call_target="tpu_custom_call" | custom-call | flops 2000000000 | bytes 10000000 | tf_op jit(solution)/shard_map/pack/pallas_call | solution.py:570
  20.8 2.8 %collective-permute-start.3 = (bf16[10240,128]{1,0:T(8,128)(2,1)}, bf16[10240,128]{1,0:T(8,128)(2,1)S(1)}, u32[]{:S(2)}, u32[]{:S(2)}) collective-permute-start(bf16[10240,128]{1,0:T(8,128)(2,1)} %get-tuple-element.32), channel_id=1, source_target_pairs={{0,1},{1,0},{2,3},{3,2},{4,5},{5,4},{6,7},{7,6},{8,9},{9,8},{10,11... | collective-permute-start | bytes 7864328 | tf_op jit(solution)/shard_map/ppermute | solution.py:527
  23.6 2.1 %collective-permute-start.4 = (bf16[5760,128]{1,0:T(8,128)(2,1)}, bf16[5760,128]{1,0:T(8,128)(2,1)}, u32[]{:S(2)}, u32[]{:S(2)}) collective-permute-start(bf16[5760,128]{1,0:T(8,128)(2,1)} %get-tuple-element.34), channel_id=1, source_target_pairs={{1,2},{2,1},{3,4},{4,3},{5,6},{6,5},{7,8},{8,7},{9,10},{10,9},{11,... | collective-permute-start | bytes 4423688 | tf_op jit(solution)/shard_map/ppermute | solution.py:527
  25.7 0.0 copy-start.3
  25.7 0.0 copy-start.4
  25.8 14.8 %own.2 = (bf16[8,320,1024]{2,1,0:T(8,128)(2,1)}, f32[4,320,320]{2,1,0:T(8,128)}) custom-call(s32[1]{0:T(128)} %bitcast.here, s32[256]{0:T(256)} %partner.11, s32[128]{0:T(128)} %convert_reduce_fusion.lens, s32[12]{0:T(128)} %get-tuple-element.24.counts, bf16[12,128,32]{2,1,0:T(8,128)(2,1)} %get-tuple-element.27.tables, s32[128,1024]{1,0:T(8,128)} %aux_rows.5, ...), custom_call_target="tpu_custom_call" | custom-call | flops 10737418240 | bytes 20000000 | tf_op jit(solution)/shard_map/own/pallas_call | solution.py:617
  40.6 0.0 copy-done.3
  40.6 0.7 copy.12.listed
  41.2 0.0 copy-done.4
  41.2 0.7 copy.13.coef
  41.9 14.6 %count.1.over = s32[1]{0:T(128)} custom-call(s32[256]{0:T(256)} %partner.11, s32[128]{0:T(128)} %convert_reduce_fusion.lens, s32[128,1024]{1,0:T(8,128)} %aux_rows.5), custom_call_target="tpu_custom_call" | custom-call | flops 1000000000 | bytes 1000000 | tf_op jit(solution)/shard_map/count/pallas_call | solution.py:599
  57.2 0.0 collective-permute-done.1.sibling
  57.2 3.5 %collective-permute-done.2.other = bf16[10,320,256]{2,1,0:T(8,128)(2,1)} collective-permute-done((bf16[10,320,256]{2,1,0:T(8,128)(2,1)}, bf16[10,320,256]{2,1,0:T(8,128)(2,1)}, u32[]{:S(2)}, u32[]{:S(2)}) %collective-permute-start.2) | collective-permute-done | bytes 1638432 | tf_op jit(solution)/shard_map/ppermute | solution.py:527
  60.6 20.7 %near.1 = (f32[8,320,320]{2,1,0:T(8,128)}, f32[4,320,320]{2,1,0:T(8,128)}) custom-call(s32[1]{0:T(128)} %bitcast.here, s32[256]{0:T(256)} %partner.11, s32[8,4]{1,0:T(8,128)} %copy.12.listed, s32[128]{0:T(128)} %convert_reduce_fusion.lens, f32[8,4]{1,0:T(8,128)} %copy.13.coef, s32[128,320]{1,0:T(8,128)} %get-tuple-element.29.pao_rows, ...), custom_call_target="tpu_custom_call" | custom-call | flops 10737418240 | bytes 20000000 | tf_op jit(solution)/shard_map/near/pallas_call | solution.py:640
  81.4 0.0 collective-permute-done.3.sibling
  81.4 0.0 copy-start
  81.4 1.5 %copy-done = bf16[10240,128]{1,0:T(8,128)(2,1)} copy-done((bf16[10240,128]{1,0:T(8,128)(2,1)}, bf16[10240,128]{1,0:T(8,128)(2,1)S(1)}, u32[]{:S(2)}) %copy-start) | copy-done | bytes 2621464
  82.9 0.0 copy-start.1
  82.9 13.3 %mid.1 = (bf16[8,320,320]{2,1,0:T(8,128)(2,1)}, f32[8]{0:T(128)}) custom-call(s32[1]{0:T(128)} %bitcast.here, s32[256]{0:T(256)} %partner.11, s32[128]{0:T(128)} %convert_reduce_fusion.lens, s32[12]{0:T(128)} %get-tuple-element.24.counts, s32[12]{0:T(128)} %get-tuple-element.25.offsets, f32[128,320]{1,0:T(8,128)} %get-tuple-element.26.gaps, ...), custom_call_target="tpu_custom_call" | custom-call | flops 1677721600 | bytes 20000000 | tf_op jit(solution)/shard_map/mid/pallas_call | solution.py:660
  96.2 0.0 collective-permute-done.4.other
  96.2 0.0 copy-done.1
  96.2 6.8 %last.1 = (bf16[8,320,320]{2,1,0:T(8,128)(2,1)}, f32[8]{0:T(128)}) custom-call(s32[1]{0:T(128)} %bitcast.here, s32[256]{0:T(256)} %partner.11, s32[128]{0:T(128)} %convert_reduce_fusion.lens, s32[12]{0:T(128)} %get-tuple-element.24.counts, s32[12]{0:T(128)} %get-tuple-element.25.offsets, s32[1]{0:T(128)} %count.1.over, ...), custom_call_target="tpu_custom_call", output_to_operand_aliasing={{0}: (13, {})} | custom-call | flops 1677721600 | bytes 20000000 | tf_op jit(solution)/shard_map/last/pallas_call | solution.py:691
  (1 shorter events, 0.0 us)
Async XLA Ops:
  0.6 6.6 %copy-start.2 = (s32[128,320]{0,1:T(8,128)S(1)}, s32[128,320]{0,1:T(8,128)}, u32[]{:S(2)}) copy-start(s32[128,320]{0,1:T(8,128)} %param.12) | copy-start | bytes 491524
  3.6 53.6 %collective-permute-start.1 = (bf16[10,320,256]{2,1,0:T(8,128)(2,1)}, bf16[10,320,256]{2,1,0:T(8,128)(2,1)}, u32[]{:S(2)}, u32[]{:S(2)}) collective-permute-start(bf16[10,320,256]{2,1,0:T(8,128)(2,1)} %slim.1), channel_id=1, source_target_pairs={{0,1},{1,0},{2,3},{3,2},{4,5},{5,4},{6,7},{7,6},{8,9},{9,8},{10,11... | collective-permute-start | bytes 4915208 | tf_op jit(solution)/shard_map/ppermute | solution.py:527
  4.2 56.4 %collective-permute-start.2 = (bf16[10,320,256]{2,1,0:T(8,128)(2,1)}, bf16[10,320,256]{2,1,0:T(8,128)(2,1)}, u32[]{:S(2)}, u32[]{:S(2)}) collective-permute-start(bf16[10,320,256]{2,1,0:T(8,128)(2,1)} %slim.1), channel_id=1, source_target_pairs={{1,2},{2,1},{3,4},{4,3},{5,6},{6,5},{7,8},{8,7},{9,10},{10,9},{11,... | collective-permute-start | bytes 4915208 | tf_op jit(solution)/shard_map/ppermute | solution.py:527
  20.8 60.6 %collective-permute-start.3 = (bf16[10240,128]{1,0:T(8,128)(2,1)}, bf16[10240,128]{1,0:T(8,128)(2,1)S(1)}, u32[]{:S(2)}, u32[]{:S(2)}) collective-permute-start(bf16[10240,128]{1,0:T(8,128)(2,1)} %get-tuple-element.32), channel_id=1, source_target_pairs={{0,1},{1,0},{2,3},{3,2},{4,5},{5,4},{6,7},{7,6},{8,9},{9,8},{10,11... | collective-permute-start | bytes 7864328 | tf_op jit(solution)/shard_map/ppermute | solution.py:527
  23.6 72.6 %collective-permute-start.4 = (bf16[5760,128]{1,0:T(8,128)(2,1)}, bf16[5760,128]{1,0:T(8,128)(2,1)}, u32[]{:S(2)}, u32[]{:S(2)}) collective-permute-start(bf16[5760,128]{1,0:T(8,128)(2,1)} %get-tuple-element.34), channel_id=1, source_target_pairs={{1,2},{2,1},{3,4},{4,3},{5,6},{6,5},{7,8},{8,7},{9,10},{10,9},{11,... | collective-permute-start | bytes 4423688 | tf_op jit(solution)/shard_map/ppermute | solution.py:527
  25.7 14.8 %copy-start.3 = (s32[8,4]{0,1:T(4,128)S(1)}, s32[8,4]{0,1:T(4,128)}, u32[]{:S(2)}) copy-start(s32[8,4]{0,1:T(4,128)} %param.16) | copy-start | bytes 388
  25.7 15.5 %copy-start.4 = (f32[8,4]{0,1:T(4,128)S(1)}, f32[8,4]{0,1:T(4,128)}, u32[]{:S(2)}) copy-start(f32[8,4]{0,1:T(4,128)} %param.17) | copy-start | bytes 388
  81.4 1.5 %copy-start = (bf16[10240,128]{1,0:T(8,128)(2,1)}, bf16[10240,128]{1,0:T(8,128)(2,1)S(1)}, u32[]{:S(2)}) copy-start(bf16[10240,128]{1,0:T(8,128)(2,1)S(1)} %collective-permute-done.3.sibling) | copy-start | bytes 7864324
  82.9 13.3 %copy-start.1 = (bf16[4480,128]{1,0:T(8,128)(2,1)S(1)}, bf16[4480,128]{1,0:T(8,128)(2,1)}, u32[]{:S(2)}) copy-start(bf16[4480,128]{1,0:T(8,128)(2,1)} %get-tuple-element.40.more) | copy-start | bytes 3440644

commit v4 on v3

--- a/solution.py
+++ b/solution.py
@@ -120,8 +120,8 @@
     return short_where(levels == jnp.broadcast_to(values.astype(jnp.bfloat16), (count, lanes)))
 
 
-def places(row, table):
-    found = dot(table, bits(row // LOW, HIGH, row.shape[1]))
+def places(row, table, k):
+    found = dot(table, bits(row // LOW + k * HIGH, table.shape[1], row.shape[1]))
     low = bits(lax.rem(row, LOW), LOW, row.shape[1]).astype(jnp.float32)
     return jnp.sum((found[:LOW] * BASE + found[LOW:]) * low, axis=0, keepdims=True)
 
@@ -145,7 +145,7 @@
 
 
 def pack_kernel(
-    s, here, partner, lens, aux_rows, blocks, pao_cols, gap_cols, to_sibling, to_other, to_other_more, tables, pao_rows, gap_rows, counts, offsets, maps, sends, bufs, sems
+    s, here, partner, lens, aux_rows, blocks, pao_cols, gap_cols, to_sibling, to_other, to_other_more, tables, pao_rows, gap_rows, counts, offsets, maps, users, sends, bufs, sems
 ):
     me = here[0]
     peers = swapped(me)
@@ -158,7 +158,9 @@
             row = aux_rows[pl.ds(orbital, 1), :]
             by_high = bits(row // LOW, HIGH, s.aux)
             by_low = bits(lax.rem(row, LOW), LOW, s.aux)
-            maps[g * s.occ + k] = dot(jnp.concatenate([by_low, by_low], axis=0), by_high, NT)
+            here_map = dot(jnp.concatenate([by_low, by_low], axis=0), by_high, NT)
+            maps[g, :, k * HIGH : (k + 1) * HIGH] = here_map
+            users[g * s.occ + k] = jnp.concatenate([here_map] * s.occ, axis=1)
             if g == 0:
                 spot = iota((LOW, s.aux), 1) + 1
                 parts = jnp.concatenate(
@@ -168,30 +170,38 @@
                     ],
                     axis=0,
                 )
-                tables[2 * s.occ + k] = dot(parts, by_high, NT).astype(jnp.bfloat16)
-
+                tables[2, :, k * HIGH : (k + 1) * HIGH] = dot(parts, by_high, NT).astype(
+                    jnp.bfloat16
+                )
+
+    wide = s.occ * HIGH
     sub, lane = iota((2 * LOW, 2 * LOW), 0), iota((2 * LOW, 2 * LOW), 1)
     ahead = one_where((lane < LOW) & (lane < lax.rem(sub, LOW)))
     first = one_where(lane < LOW)
-    above = one_where(iota((HIGH, HIGH), 0) < iota((HIGH, HIGH), 1))
-    level = iota((2 * LOW, HIGH), 0)
-
-    def listing(target, users, device, orbital):
-        union = jnp.zeros((2 * LOW, HIGH), jnp.float32)
+    sub, lane = iota((wide, wide), 0), iota((wide, wide), 1)
+    above = one_where((sub // HIGH == lane // HIGH) & (sub < lane))
+    level = iota((2 * LOW, wide), 0)
+    owner = iota((1, wide), 1) // HIGH
+
+    def listing(target, target_device, user, user_device):
+        union = jnp.zeros((2 * LOW, wide), jnp.float32)
         for q in range(s.occ):
-            uses = jnp.bool_(False)
+            uses = jnp.zeros((1, wide), jnp.float32)
             for pair in range(q, s.pairs, s.occ):
-                pair += device * s.pairs
+                pair += user_device * s.pairs
                 inside = (pair >= 0) & (pair < s.npair)
-                uses |= inside & (partner[jnp.clip(pair, 0, s.npair - 1)] == orbital)
-            union += jnp.where(uses, 1.0, 0.0) * maps[users + q]
+                k = partner[jnp.clip(pair, 0, s.npair - 1)] - target_device * s.occ
+                uses += jnp.where((owner == k) & inside, 1.0, 0.0)
+            union += uses * users[user * s.occ + q]
         taken = (union > 0.0) & (maps[target] > 0.0)
         flags = one_where(taken)
         total = dot(first, flags)
         place = dot(ahead, flags) + dot(total.astype(jnp.bfloat16), above) + 1.0
         place = jnp.where(taken, place, 0.0).astype(jnp.int32)
-        count = jnp.sum(total[:1]).astype(jnp.int32)
-        return split_place(place, level), count
+        found = [
+            jnp.sum(jnp.where(owner == k, total[:1], 0.0)).astype(jnp.int32) for k in range(s.occ)
+        ]
+        return split_place(place, level), found
 
     copies = {
         0: [pltpu.make_async_copy(bufs.at[0, pl.ds(0, s.rows)], to_sibling, sems.at[0])],
@@ -203,18 +213,14 @@
         ],
     }
     for r in (1, 0):
-        listed = []
+        sends[r], found = listing(0, me, 1 + r, peers[r])
         at = jnp.int32(0)
-        for k in range(s.occ):
-            sends[k], count = listing(k, (1 + r) * s.occ, peers[r], me * s.occ + k)
+        for k, count in enumerate(found):
             step = rows_of(lens[me * s.occ + k])
-            listed.append((at, step, count))
-            at += chunks_of(count) * step
-        for k, (at, step, count) in enumerate(listed):
 
             @pl.when(count > 0)
             def _(k=k, at=at, step=step, count=count):
-                place = places(aux_rows[pl.ds(me * s.occ + k, 1), :], sends[k])
+                place = places(aux_rows[pl.ds(me * s.occ + k, 1), :], sends[r], k)
 
                 def some(c):
                     got = dot(blocks[k], picker(place, c), NT).astype(jnp.bfloat16)
@@ -227,17 +233,19 @@
 
                 chunkwise(s, count, some)
 
+            at += chunks_of(count) * step
+
         for copy in copies[r]:
             copy.start()
 
     for r in range(2):
+        tables[r], found = listing(1 + r, peers[r], 0, me)
         at = jnp.int32(0)
-        for k in range(s.occ):
-            l = r * s.occ + k
+        for k, count in enumerate(found):
             orbital = jnp.clip(peers[r] * s.occ + k, 0, s.nocc - 1)
-            tables[l], counts[l] = listing((1 + r) * s.occ + k, 0, me, peers[r] * s.occ + k)
-            offsets[l] = at
-            at += chunks_of(counts[l]) * rows_of(lens[orbital])
+            counts[r * s.occ + k] = count
+            offsets[r * s.occ + k] = at
+            at += chunks_of(count) * rows_of(lens[orbital])
     for k in range(s.occ):
         counts[2 * s.occ + k] = jnp.int32(s.aux)
         offsets[2 * s.occ + k] = jnp.int32(0)
@@ -246,100 +254,92 @@
         copy.wait()
 
 
-def count_kernel(s, partner, lens, aux_rows, over, maps, sums, steps):
-    high = AUX_IDS // LANES
-    group = 8
-
-    def some(g, _):
-        rows = aux_rows[pl.ds(pl.multiple_of(g * group, group), group), :]
-        for t in range(group):
-            row = rows[t : t + 1]
-            by_low = bits(lax.rem(row, LANES), LANES, s.aux)
-            maps[g * group + t] = dot(bits(row // LANES, high, s.aux), by_low, NT)
-        return 0
-
-    lax.fori_loop(0, s.nocc // group, some, 0)
-
-    sums[...] = jnp.zeros_like(sums)
-    steps[...] = jnp.zeros_like(steps)
+def count_kernel(s, partner, lens, aux_rows, over):
     devices = s.nocc // s.occ
+    full = s.aux // LANES
+
+    def ids(orbital):
+        row = aux_rows[pl.ds(orbital, 1), :]
+        return dot(bits(row // LOW, HIGH, s.aux), bits(lax.rem(row, LOW), LOW, s.aux), NT)
+
+    over[0] = jnp.int32(0)
 
     def edge(e, _):
         source = e + 1
         user = source + 1 - 2 * lax.rem(e, 2)
+        reads = [partner[user * s.pairs + q] - source * s.occ for q in range(s.pairs)]
+        bound = jnp.int32(0)
         for k in range(s.occ):
-            orbital = source * s.occ + k
-            union = jnp.zeros((high, LANES), jnp.float32)
-            for q in range(s.occ):
-                uses = jnp.bool_(False)
-                for pair in range(q, s.pairs, s.occ):
-                    uses |= partner[user * s.pairs + pair] == orbital
-                union += jnp.where(uses, 1.0, 0.0) * maps[user * s.occ + q]
-            taken = jnp.where((union > 0.0) & (maps[orbital] > 0.0), 1.0, 0.0)
-            sums[k, pl.ds(e, 1), :] = jnp.sum(taken, axis=0, keepdims=True)
-            steps[k, pl.ds(e, 1), :] = jnp.full(
-                (1, LANES), rows_of(lens[orbital]).astype(jnp.float32), jnp.float32
-            )
+            used = functools.reduce(jnp.logical_or, [read == k for read in reads])
+            bound += jnp.where(used, full * rows_of(lens[source * s.occ + k]), 0)
+
+        @pl.when(bound > s.first)
+        def _():
+            domains = [ids(user * s.occ + q) for q in range(s.occ)]
+            need = jnp.int32(0)
+            for k in range(s.occ):
+                union = jnp.zeros((HIGH, LOW), jnp.float32)
+                for q, domain in enumerate(domains):
+                    used = functools.reduce(
+                        jnp.logical_or, [read == k for read in reads[q :: s.occ]]
+                    )
+                    union += jnp.where(used, 1.0, 0.0) * domain
+                taken = (union > 0.0) & (ids(source * s.occ + k) > 0.0)
+                count = jnp.sum(jnp.where(taken, 1.0, 0.0)).astype(jnp.int32)
+                need += chunks_of(count) * rows_of(lens[source * s.occ + k])
+            over[0] = jnp.maximum(over[0], (need > s.first).astype(jnp.int32))
+
         return 0
 
     lax.fori_loop(0, devices - 2, edge, 0)
-    need = jnp.zeros(sums.shape[1:], jnp.float32)
-    ones = jnp.ones((LANES, LANES), jnp.bfloat16)
-    for k in range(s.occ):
-        count = dot(sums[k].astype(jnp.bfloat16), ones)
-        need += jnp.floor((count + (LANES - 1)) / LANES) * steps[k]
-    over[0] = (jnp.max(need) > s.first).astype(jnp.int32)
 
 
 def own_kernel(s, here, partner, lens, counts, tables, aux_rows, blocks, amps, aligned, dens):
-    g = pl.program_id(0)
+    left = pl.program_id(0)
     me = here[0]
-    left, p = paired(s, g)
-    right = partner[me * s.pairs + p]
-    l, _ = s.where_partner(me, right)
-    count = counts[l]
-    place = places(aux_rows[pl.ds(me * s.occ + left, 1), :], tables[l])
     wide = 2 * LANES
-
-    def some(c):
-        aligned[0, :, c * wide : (c + 1) * wide] = dot(
-            blocks[0], picker(place, c), NT
-        ).astype(jnp.bfloat16)
-
     chunks = s.aux // wide
-    for c in range(chunks - 1):
-        some(c)
-    pl.when(count > (chunks - 1) * wide)(functools.partial(some, chunks - 1))
-
-    masked = kept(amps[0], lens[me * s.occ + left], lens[right])
-    term = dot(masked, masked, NT)
-
-    @pl.when(lax.rem(g, s.pairs // s.occ) == 0)
-    def _():
-        dens[0] = term
-
-    @pl.when(lax.rem(g, s.pairs // s.occ) != 0)
-    def _():
-        dens[0] += term
-
-
-def paired(s, g):
-    repeats = s.pairs // s.occ
-    left = g // repeats
-    return left, lax.rem(g, repeats) * s.occ + left
-
-
-def near_kernel(
-    s, ncpl, here, partner, listed, lens, coef, pao_rows, sibling, own, other, dens_in, coupling, dens, wide, tall, dens_own, sem
+    row = aux_rows[pl.ds(me * s.occ + left, 1), :]
+    term = jnp.zeros((s.pao, s.pao), jnp.float32)
+    rest = []
+
+    for t in range(s.pairs // s.occ):
+        right = partner[me * s.pairs + t * s.occ + left]
+        l, kind = s.where_partner(me, right)
+        place = places(row, tables[kind], lax.rem(right, s.occ))
+
+        def some(c, t=t, place=place):
+            aligned[t, 0, :, c * wide : (c + 1) * wide] = dot(
+                blocks[0], picker(place, c), NT
+            ).astype(jnp.bfloat16)
+
+        for c in range(chunks - 1):
+            some(c)
+        rest.append((counts[l] > (chunks - 1) * wide, functools.partial(some, chunks - 1)))
+        masked = kept(amps[t, 0], lens[me * s.occ + left], lens[right])
+        term += dot(masked, masked, NT)
+
+    dens[0] = term
+    for needed, act in rest:
+        pl.when(needed)(act)
+
+
+def main_kernel(
+    s, ncpl, here, partner, listed, lens, coef, counts, offsets, pao_rows, gaps, sibling, own, other, aligned, dens_in, blocks, from_sibling, coupling, dens, new_amps, energy, wide, tall, dens_own, near_blocks, halo, sums, sems
 ):
     p = pl.program_id(0)
     me = here[0]
     peers = swapped(me)
-    fetch = pltpu.make_async_copy(dens_in, dens_own, sem)
+    fetches = [
+        pltpu.make_async_copy(from_sibling, halo.at[pl.ds(0, s.rows), :], sems.at[0]),
+        pltpu.make_async_copy(blocks, near_blocks, sems.at[1]),
+        pltpu.make_async_copy(dens_in, dens_own, sems.at[2]),
+    ]
 
     @pl.when(p == 0)
     def _():
-        fetch.start()
+        for fetch in fetches:
+            fetch.start()
         dens[...] = jnp.zeros_like(dens)
         wide[s.pairs : 2 * s.pairs] = own[...]
         for device, packed in zip(peers, (sibling, other)):
@@ -357,11 +357,11 @@
     left_col = column_of(me * s.occ + lax.rem(p, s.occ))
     left_rows = []
     for c in range(ncpl):
-        m = listed[p, c]
+        m = listed[c, p]
         left_rows.append(row_of(s.first_orbital(m)))
         amp = wide[m - (me - 1) * s.pairs]
         moved = dot(amp, same(right_col, row_of(partner[m]).astype(jnp.int16)), NT)
-        tall[c * s.pao : (c + 1) * s.pao] = (coef[p, c] * moved).astype(jnp.bfloat16)
+        tall[c * s.pao : (c + 1) * s.pao] = (coef[c, p] * moved).astype(jnp.bfloat16)
     left_row = jnp.concatenate(left_rows, axis=1).astype(jnp.int16)
     coupling[0] = dot(same(left_col, left_row), tall[...])
 
@@ -377,25 +377,56 @@
             masked = kept(amp, lens[s.first_orbital(m)], lens[partner[m]])
             dens[near] += dot(masked, masked, TN)
 
+    @pl.when(p == 0)
+    def _():
+        for fetch in fetches:
+            fetch.wait()
+
+    left, right = me * s.occ + lax.rem(p, s.occ), partner[me * s.pairs + p]
+    l, kind = s.where_partner(me, right)
+
+    @pl.when(kind == 2)
+    def _():
+        sums[...] = dot(aligned[0], near_blocks[lax.rem(right, s.occ)], NT)
+
+    @pl.when(kind == 0)
+    def _():
+        compacted(s, counts[l], offsets[l], rows_of(lens[right]), aligned.at[0], halo, sums)
+
+    @pl.when(kind != 1)
+    def _():
+        new_amps[0], energy[p] = update(
+            s, lens[left], lens[right], sums[...], own[p], coupling[0], gaps[pl.ds(left, 1), :], gaps[pl.ds(right, 1), :]
+        )
+
+    @pl.when(kind == 1)
+    def _():
+        energy[p] = 0.0
+
     @pl.when(p == s.pairs - 1)
     def _():
-        fetch.wait()
-        dens[...] = (dens[...] + dens_own[...]) / s.pao
+        dens[...] = (dens[...] + dens_own[...]) * (1.0 / s.pao)
 
 
 def update(s, lens_left, lens_right, exchange, amp, coupling, gap_left, gap_right):
-    mask = live(lens_left, lens_right, (s.pao, s.pao))
-    exchange = jnp.where(mask, exchange, 0.0)
-    masked = jnp.where(mask, amp.astype(jnp.float32), 0.0)
     left = column(gap_left)
     parts = []
+    energy = jnp.zeros((s.pao, LANES), jnp.float32)
     for at in range(0, s.pao, LANES):
         lanes = slice(at, min(at + LANES, s.pao))
-        part = masked[:, lanes]
-        denom = left[:, : part.shape[1]] + gap_right[:, lanes]
-        residual = exchange[:, lanes] + denom * part - coupling[:, lanes]
-        parts.append((part - 0.5 * residual / denom).astype(jnp.bfloat16))
-    return jnp.concatenate(parts, axis=1), jnp.sum(exchange * masked) / s.pao
+        part = amp[:, lanes].astype(jnp.float32)
+        shape = part.shape
+        mask = live(lens_left, lens_right - at, shape)
+        denom = left[:, : shape[1]] + gap_right[:, lanes]
+        inverse = pl.reciprocal(denom, approx=True)
+        inverse = inverse * (2.0 - denom * inverse)
+        moved = (exchange[:, lanes] - coupling[:, lanes]) * inverse
+        parts.append(jnp.where(mask, 0.5 * (part - moved), 0.0).astype(jnp.bfloat16))
+        term = jnp.where(mask, exchange[:, lanes] * part, 0.0)
+        if shape[1] < LANES:
+            term = jnp.concatenate([term, jnp.zeros((s.pao, LANES - shape[1]), jnp.float32)], axis=1)
+        energy += term
+    return jnp.concatenate(parts, axis=1), jnp.sum(energy) / s.pao
 
 
 def compacted(s, count, at, step, aligned, halo, sums):
@@ -418,40 +449,6 @@
         sums[...] = jnp.zeros_like(sums)
 
     chunkwise(s, count, some)
-
-
-def mid_kernel(
-    s, here, partner, lens, counts, offsets, gaps, aligned, coupling, amps, own, sibling, new_amps, energy, halo, sums, sem
-):
-    p = pl.program_id(0)
-    me = here[0]
-    left, right = me * s.occ + lax.rem(p, s.occ), partner[me * s.pairs + p]
-    l, kind = s.where_partner(me, right)
-
-    @pl.when(p == 0)
-    def _():
-        copy = pltpu.make_async_copy(sibling, halo.at[pl.ds(0, s.rows), :], sem)
-        copy.start()
-        copy.wait()
-
-    @pl.when(kind == 2)
-    def _():
-        sums[...] = dot(aligned[0], own[lax.rem(right, s.occ)], NT)
-
-    @pl.when(kind == 0)
-    def _():
-        compacted(s, counts[l], offsets[l], rows_of(lens[right]), aligned.at[0], halo, sums)
-
-    @pl.when(kind != 1)
-    def _():
-        new_amps[0], energy[p] = update(
-            s, lens[left], lens[right], sums[...], amps[0], coupling[0], gaps[pl.ds(left, 1), :], gaps[pl.ds(right, 1), :]
-        )
-
-    @pl.when(kind == 1)
-    def _():
-        new_amps[0] = jnp.zeros_like(amps[0])
-        energy[p] = 0.0
 
 
 def last_kernel(
@@ -575,15 +572,16 @@
             jax.ShapeDtypeStruct((s.rows, LANES), jnp.bfloat16),
             jax.ShapeDtypeStruct((s.first, LANES), jnp.bfloat16),
             jax.ShapeDtypeStruct((s.rows - s.first, LANES), jnp.bfloat16),
-            jax.ShapeDtypeStruct((lists, 2 * LOW, HIGH), jnp.bfloat16),
+            jax.ShapeDtypeStruct((3, 2 * LOW, s.occ * HIGH), jnp.bfloat16),
             jax.ShapeDtypeStruct(pao_domain.shape, pao_domain.dtype),
             jax.ShapeDtypeStruct(pao_gap.shape, pao_gap.dtype),
             jax.ShapeDtypeStruct((lists,), jnp.int32),
             jax.ShapeDtypeStruct((lists,), jnp.int32),
         ],
         scratch_shapes=[
-            pltpu.VMEM((3 * s.occ, 2 * LOW, HIGH), jnp.float32),
-            pltpu.VMEM((s.occ, 2 * LOW, HIGH), jnp.bfloat16),
+            pltpu.VMEM((3, 2 * LOW, s.occ * HIGH), jnp.float32),
+            pltpu.VMEM((3 * s.occ, 2 * LOW, s.occ * HIGH), jnp.float32),
+            pltpu.VMEM((2, 2 * LOW, s.occ * HIGH), jnp.bfloat16),
             pltpu.VMEM((2, s.rows + s.pao, LANES), jnp.bfloat16),
             pltpu.SemaphoreType.DMA((3,)),
         ],
@@ -595,96 +593,71 @@
     from_other = swap(to_other, 1)
     from_sibling = swap(to_sibling, 0)
 
-    edges = -(-(s.nocc // s.occ) // 8) * 8
     (over,) = pl.pallas_call(
         functools.partial(count_kernel, s),
         in_specs=[smem] * 2 + [vmem],
         out_specs=[smem],
         out_shape=[jax.ShapeDtypeStruct((1,), jnp.int32)],
-        scratch_shapes=[
-            pltpu.VMEM((s.nocc, AUX_IDS // LANES, LANES), jnp.float32),
-            pltpu.VMEM((s.occ, edges, LANES), jnp.float32),
-            pltpu.VMEM((s.occ, edges, LANES), jnp.float32),
-        ],
         compiler_params=plain,
         cost_estimate=cost(10**9, 10**6),
         name="count",
     )(pair_partner, lens, aux_domain)
 
-    def by_left(block):
-        return pl.BlockSpec((1,) + block, lambda g: (paired(s, g)[0], 0, 0))
-
+    repeats = s.pairs // s.occ
+    both = pl.BlockSpec((repeats, 1, s.pao, s.aux), lambda g: (0, g, 0, 0))
     aligned, dens = pl.pallas_call(
         functools.partial(own_kernel, s),
-        grid=(s.pairs,),
+        grid=(s.occ,),
         in_specs=[smem] * 4
         + [
             vmem,
             vmem,
-            by_left((s.pao, s.aux)),
-            pl.BlockSpec((1, s.pao, s.pao), lambda g: (paired(s, g)[1], 0, 0)),
-        ],
-        out_specs=[
-            pl.BlockSpec((1, s.pao, s.aux), lambda g: (paired(s, g)[1], 0, 0)),
-            by_left((s.pao, s.pao)),
-        ],
+            pl.BlockSpec((1, s.pao, s.aux), lambda g: (g, 0, 0)),
+            pl.BlockSpec((repeats, 1, s.pao, s.pao), lambda g: (0, g, 0, 0)),
+        ],
+        out_specs=[both, pl.BlockSpec((1, s.pao, s.pao), lambda g: (g, 0, 0))],
         out_shape=[
-            jax.ShapeDtypeStruct((s.pairs, s.pao, s.aux), jnp.bfloat16),
+            jax.ShapeDtypeStruct((repeats, s.occ, s.pao, s.aux), jnp.bfloat16),
             dens_shape,
         ],
         compiler_params=stepped,
         cost_estimate=cost(2 * s.pairs * s.pao * s.aux * s.aux * 2, 2 * 10**7),
         name="own",
-    )(here, pair_partner, lens, counts, tables, aux_domain, blocks_t, amplitudes)
-
-    coupling, densities = pl.pallas_call(
-        functools.partial(near_kernel, s, ncpl),
+    )(
+        here, pair_partner, lens, counts, tables, aux_domain, blocks_t,
+        amplitudes.reshape(repeats, s.occ, s.pao, s.pao),
+    )
+    aligned = aligned.reshape(s.pairs, s.pao, s.aux)
+
+    coupling, densities, some_amps, some_energies = pl.pallas_call(
+        functools.partial(main_kernel, s, ncpl),
         grid=(s.pairs,),
-        in_specs=[smem] * 5 + [vmem] * 4 + [anywhere],
-        out_specs=[square, all_dens],
-        out_shape=[squares, dens_shape],
+        in_specs=[smem] * 7
+        + [vmem] * 5
+        + [pl.BlockSpec((1, s.pao, s.aux), lambda p: (p, 0, 0))]
+        + [anywhere] * 3,
+        out_specs=[square, all_dens, square, smem],
+        out_shape=[
+            squares,
+            dens_shape,
+            jax.ShapeDtypeStruct(amplitudes.shape, amplitudes.dtype),
+            jax.ShapeDtypeStruct((s.pairs,), jnp.float32),
+        ],
         scratch_shapes=[
             pltpu.VMEM((3 * s.pairs, s.pao, s.pao), jnp.bfloat16),
             pltpu.VMEM((ncpl * s.pao, s.pao), jnp.bfloat16),
             pltpu.VMEM((s.occ, s.pao, s.pao), jnp.float32),
-            pltpu.SemaphoreType.DMA,
+            pltpu.VMEM((s.occ, s.pao, s.aux), jnp.bfloat16),
+            pltpu.VMEM((s.rows + s.pao, LANES), jnp.bfloat16),
+            pltpu.VMEM((s.pao, s.pao), jnp.float32),
+            pltpu.SemaphoreType.DMA((3,)),
         ],
         compiler_params=stepped,
         cost_estimate=cost(2 * s.pairs * s.pao * s.aux * s.aux * 2, 2 * 10**7),
-        name="near",
+        name="main",
     )(
-        here, pair_partner, coupling_list, lens, coupling_coef,
-        pao_rows, amps_sibling, amplitudes, amps_other, dens,
-    )
-
-    some_amps, some_energies = pl.pallas_call(
-        functools.partial(mid_kernel, s),
-        grid=(s.pairs,),
-        in_specs=[smem] * 5
-        + [
-            vmem,
-            pl.BlockSpec((1, s.pao, s.aux), lambda p: (p, 0, 0)),
-            square,
-            square,
-            vmem,
-            anywhere,
-        ],
-        out_specs=[square, smem],
-        out_shape=[
-            jax.ShapeDtypeStruct(amplitudes.shape, amplitudes.dtype),
-            jax.ShapeDtypeStruct((s.pairs,), jnp.float32),
-        ],
-        scratch_shapes=[
-            pltpu.VMEM((s.rows + s.pao, LANES), jnp.bfloat16),
-            pltpu.VMEM((s.pao, s.pao), jnp.float32),
-            pltpu.SemaphoreType.DMA,
-        ],
-        compiler_params=stepped,
-        cost_estimate=cost(2 * s.pairs * s.pao * s.pao * s.aux, 2 * 10**7),
-        name="mid",
-    )(
-        here, pair_partner, lens, counts, offsets,
-        gap_rows, aligned, coupling, amplitudes, blocks_t, from_sibling,
+        here, pair_partner, coupling_list.T, lens, coupling_coef.T, counts, offsets,
+        pao_rows, gap_rows, amps_sibling, amplitudes, amps_other, aligned, dens, blocks_t, from_sibling,
     )
 
     from_other_more = lax.cond(over[0] > 0, lambda a: swap(a, 1), lambda a: a, to_other_more)

time: 105 us -> 112 us (1.067)
  the two profiles are of different devices: /device:TPU:21 before, /device:TPU:1 now
where the time goes in v4:
time: 112 us; the launch traced here: 111 us
  Pallas kernels  63.8 us (57%)
  waiting for transfers between devices  29.8 us (27%)
  starting transfers between devices  13.7 us (12%)
  between operations  1.5 us (1%)
  other arithmetic  1.49 us (1%)
    ppermute x4, waiting for transfers between devices, swap(): return lax.ppermute(array, AXES, route)  29.8 us
    pallas_call x1, Pallas kernels, local(): pl.pallas_call(functools.partial(main_kernel, s, ncpl), grid=(s.pairs,),...  26.6 us
    ppermute x4, starting transfers between devices, swap(): return lax.ppermute(array, AXES, route)  13.7 us
    pallas_call x1, Pallas kernels, local(): pl.pallas_call(functools.partial(own_kernel, s), grid=(s.occ,), in_specs=...  12.5 us
    pallas_call x1, Pallas kernels, local(): pl.pallas_call(functools.partial(pack_kernel, s), in_specs=[smem] * 3 + [...  9.3 us
    pallas_call x1, Pallas kernels, local(): pl.pallas_call(functools.partial(last_kernel, s), in_specs=[smem] * 7 + [...  6.98 us
    pallas_call x1, Pallas kernels, local(): pl.pallas_call(functools.partial(count_kernel, s), in_specs=[smem] * 2 +...  5.58 us
    pallas_call x1, Pallas kernels, local(): pl.pallas_call(functools.partial(slim_kernel, s), in_specs=[vmem], out_sp...  2.89 us
  transfers between devices with their start and end apart: 4, of which 1 were waited for; matrix products, arithmetic and copies ran while one was open for 0% of the time, Pallas kernels for 43%

profile of v4, /device:TPU:1, one launch (start us, length us, event | category | flops | bytes accessed | tf_op | source)
XLA Modules:
  0.0 111.5 jit_solution(18359843191987019868)
XLA Ops:
  0.6 1.5 %convert_reduce_fusion.lens = s32[128]{0:T(128)} fusion(s32[128,320]{0,1:T(8,128)} %param.12), kind=kLoop, calls=%fused_computation | loop fusion | flops 122752 | bytes 164352 | tf_op jit(solution)/shard_map/reduce_sum | solution.py:564
  2.1 9.3 %pack.1 = (bf16[10240,128]{1,0:T(8,128)(2,1)}, bf16[5760,128]{1,0:T(8,128)(2,1)}, bf16[4480,128]{1,0:T(8,128)(2,1)S(1)}, bf16[3,128,128]{2,1,0:T(8,128)(2,1)}, s...) custom-call(s32[1]{0:T(128)} %bitcast.here, s32[256]{0:T(256)} %partner.9, ...), custom_call_target="tpu_custom_call" | custom-call | flops 2000000000 | bytes 10000000 | tf_op jit(solution)/shard_map/pack/pallas_call | solution.py:567
  11.4 0.1 collective-permute-start.3
  11.5 2.9 %slim.1 = bf16[10,320,256]{2,1,0:T(8,128)(2,1)} custom-call(bf16[8,320,320]{2,1,0:T(8,128)(2,1)} %amps.3), custom_call_target="tpu_custom_call" | custom-call | flops 1000000 | bytes 4000000 | tf_op jit(solution)/shard_map/slim/pallas_call | solution.py:552
  14.4 0.5 collective-permute-start.1
  14.9 11.1 %collective-permute-start.2 = (bf16[10,320,256]{2,1,0:T(8,128)(2,1)}, bf16[10,320,256]{2,1,0:T(8,128)(2,1)}, u32[]{:S(2)}, u32[]{:S(2)}) collective-permute-start(bf16[10,320,256]{2,1,0:T(8,128)(2,1)} %slim.1), channel_id=1, source_target_pairs={{1,2},{2,1},{3,4},{4,3},{5,6},{6,5},{7,8},{8,7},{9,10},{10,9},{11,... | collective-permute-start | bytes 4915208 | tf_op jit(solution)/shard_map/ppermute | solution.py:524
  26.0 2.1 %collective-permute-start.4 = (bf16[5760,128]{1,0:T(8,128)(2,1)}, bf16[5760,128]{1,0:T(8,128)(2,1)S(1)}, u32[]{:S(2)}, u32[]{:S(2)}) collective-permute-start(bf16[5760,128]{1,0:T(8,128)(2,1)} %get-tuple-element.34), channel_id=1, source_target_pairs={{1,2},{2,1},{3,4},{4,3},{5,6},{6,5},{7,8},{8,7},{9,10},{10,9},{11,... | collective-permute-start | bytes 4423688 | tf_op jit(solution)/shard_map/ppermute | solution.py:524
  28.1 12.5 %own.2 = (bf16[2,4,320,1024]{3,2,1,0:T(8,128)(2,1)}, f32[4,320,320]{2,1,0:T(8,128)}) custom-call(s32[1]{0:T(128)} %bitcast.here, s32[256]{0:T(256)} %partner.9, s32[128]{0:T(128)} %convert_reduce_fusion.lens, s32[12]{0:T(128)} %get-tuple-element.24.counts, bf16[3,128,128]{2,1,0:T(8,128)(2,1)} %get-tuple-element.28.tables, s32[128,1024]{1,0:T(8,128)} %aux_rows.5, ...), custom_call_target="tpu_custom_call" | custom-call | flops 10737418240 | bytes 20000000 | tf_op jit(solution)/shard_map/own/pallas_call | solution.py:608
  40.6 5.6 %count.1.over = s32[1]{0:T(128)} custom-call(s32[256]{0:T(256)} %partner.9, s32[128]{0:T(128)} %convert_reduce_fusion.lens, s32[128,1024]{1,0:T(8,128)} %aux_rows.5), custom_call_target="tpu_custom_call" | custom-call | flops 1000000000 | bytes 1000000 | tf_op jit(solution)/shard_map/count/pallas_call | solution.py:596
  46.9 0.0 collective-permute-done.1.sibling
  46.9 29.8 %collective-permute-done.2.other = bf16[10,320,256]{2,1,0:T(8,128)(2,1)} collective-permute-done((bf16[10,320,256]{2,1,0:T(8,128)(2,1)}, bf16[10,320,256]{2,1,0:T(8,128)(2,1)}, u32[]{:S(2)}, u32[]{:S(2)}) %collective-permute-start.2) | collective-permute-done | bytes 1638432 | tf_op jit(solution)/shard_map/ppermute | solution.py:524
  76.7 0.0 collective-permute-done.3.from_sibling
  76.7 26.6 %main.1 = (f32[8,320,320]{2,1,0:T(8,128)}, f32[4,320,320]{2,1,0:T(8,128)}, bf16[8,320,320]{2,1,0:T(8,128)(2,1)}, f32[8]{0:T(128)}) custom-call(s32[1]{0:T(128)} %bitcast.here, s32[256]{0:T(256)} %partner.9, s32[4,8]{1,0:T(4,128)} %bitcast.17, s32[128]{0:T(128)} %convert_reduce_fusion.lens, f32[4,8]{1,0:T(4,128)} %bitcast.18, s32[12]{0:T(128)} %get-tuple-element.24.counts, ...), custom_call_target="tpu_custom_call" | custom-call | flops 10737418240 | bytes 20000000 | tf_op jit(solution)/shard_map/main/pallas_call | solution.py:632
  103.2 0.0 collective-permute-done.4.other
  103.2 0.0 copy-start
  103.2 1.1 copy-done
  104.4 7.0 %last.1 = (bf16[8,320,320]{2,1,0:T(8,128)(2,1)}, f32[8]{0:T(128)}) custom-call(s32[1]{0:T(128)} %bitcast.here, s32[256]{0:T(256)} %partner.9, s32[128]{0:T(128)} %convert_reduce_fusion.lens, s32[12]{0:T(128)} %get-tuple-element.24.counts, s32[12]{0:T(128)} %get-tuple-element.25.offsets, s32[1]{0:T(128)} %count.1.over, ...), custom_call_target="tpu_custom_call", output_to_operand_aliasing={{0}: (13, {})} | custom-call | flops 1677721600 | bytes 20000000 | tf_op jit(solution)/shard_map/last/pallas_call | solution.py:664
  (1 shorter events, 0.0 us)
Async XLA Ops:
  11.4 65.2 %collective-permute-start.3 = (bf16[10240,128]{1,0:T(8,128)(2,1)}, bf16[10240,128]{1,0:T(8,128)(2,1)}, u32[]{:S(2)}, u32[]{:S(2)}) collective-permute-start(bf16[10240,128]{1,0:T(8,128)(2,1)} %get-tuple-element.31), channel_id=1, source_target_pairs={{0,1},{1,0},{2,3},{3,2},{4,5},{5,4},{6,7},{7,6},{8,9},{9,8},{10,11... | collective-permute-start | bytes 7864328 | tf_op jit(solution)/shard_map/ppermute | solution.py:524
  14.4 32.5 %collective-permute-start.1 = (bf16[10,320,256]{2,1,0:T(8,128)(2,1)}, bf16[10,320,256]{2,1,0:T(8,128)(2,1)}, u32[]{:S(2)}, u32[]{:S(2)}) collective-permute-start(bf16[10,320,256]{2,1,0:T(8,128)(2,1)} %slim.1), channel_id=1, source_target_pairs={{0,1},{1,0},{2,3},{3,2},{4,5},{5,4},{6,7},{7,6},{8,9},{9,8},{10,11... | collective-permute-start | bytes 4915208 | tf_op jit(solution)/shard_map/ppermute | solution.py:524
  14.9 61.8 %collective-permute-start.2 = (bf16[10,320,256]{2,1,0:T(8,128)(2,1)}, bf16[10,320,256]{2,1,0:T(8,128)(2,1)}, u32[]{:S(2)}, u32[]{:S(2)}) collective-permute-start(bf16[10,320,256]{2,1,0:T(8,128)(2,1)} %slim.1), channel_id=1, source_target_pairs={{1,2},{2,1},{3,4},{4,3},{5,6},{6,5},{7,8},{8,7},{9,10},{10,9},{11,... | collective-permute-start | bytes 4915208 | tf_op jit(solution)/shard_map/ppermute | solution.py:524
  26.0 77.2 %collective-permute-start.4 = (bf16[5760,128]{1,0:T(8,128)(2,1)}, bf16[5760,128]{1,0:T(8,128)(2,1)S(1)}, u32[]{:S(2)}, u32[]{:S(2)}) collective-permute-start(bf16[5760,128]{1,0:T(8,128)(2,1)} %get-tuple-element.34), channel_id=1, source_target_pairs={{1,2},{2,1},{3,4},{4,3},{5,6},{6,5},{7,8},{8,7},{9,10},{10,9},{11,... | collective-permute-start | bytes 4423688 | tf_op jit(solution)/shard_map/ppermute | solution.py:524
  103.2 1.1 %copy-start = (bf16[5760,128]{1,0:T(8,128)(2,1)}, bf16[5760,128]{1,0:T(8,128)(2,1)S(1)}, u32[]{:S(2)}) copy-start(bf16[5760,128]{1,0:T(8,128)(2,1)S(1)} %collective-permute-done.4.other) | copy-start | bytes 4423684
